TPU v7x, 32 devices: a whole 2x2x4 slice. The times are simulated.
32 devices in a mesh: dp: 4 (over z), expert: 8 (over y, x, core).
Axes of the slice: x: 2, y: 2, z: 4, core: 2. Of those that a mesh axis runs over, the one named last changes fastest.
Arguments:
- hidden: bfloat16 [32768, 768], P(('dp', 'expert')), may hold values from -6 to 6
- grad_out: bfloat16 [32768, 2048], P(('dp', 'expert')), may hold values from -0.19921875 to 0.19921875
- block_slot: int32 [32, 8], P(('dp', 'expert')), may hold values from 0 to 2, as said below
- block_count: int32 [32], P(('dp', 'expert')), may hold values from 2 to 8, as said below
- replica_expert: int32 [8], replicated, may hold values from 0 to 15, as said below
Outputs:
- grad_down: bfloat16 [16, 768, 2048], P('expert', None, 'dp')
Inputs may be any that keep to these rules, and one draw needn't show every extreme that they name: `replica_expert`: Expert-axis index k is home to experts k * 2 to k * 2 + 1 and has one replica slot. The indices holding an expert homed at h are h alone, or h and (h + 4) mod 8, or h and (h + m * 2) mod 8 for m = 1, 2, 3; in every draw some expert homed at index 7 has such a set of four. `block_count`: some device has all 8 blocks live. `block_slot`: block 0 of every device belongs to the replica slot 2.
All inputs are finite; a program needn't handle non-finite values.
Results may differ from a plain program's by a relative error of at most 0.0065.
Values may be sent and summed in bfloat16 or wider, within the bound.
No kernel may reach another device: no remote copies, remote signals or barrier semaphores. Data moves between devices by JAX's collectives and lax.ppermute only.
A program may use at most 128 MiB of HBM per device.

v0:
```python
import jax
import jax.numpy as jnp
from jax import lax
from jax.sharding import PartitionSpec as P

EXP_DEV = 2
BLOCKS = 8


def from_behind(block, axis, distance):
    devices = range(lax.axis_size(axis))
    route = [((i - distance) % len(devices), i) for i in devices]
    return lax.ppermute(block, axis, route)


def slot_products(hidden, grad_out, slot_of, block_live):
    block_total = slot_of.shape[0]
    rows_per = hidden.shape[0] // block_total
    results = []
    for slot in range(EXP_DEV + 1):
        chosen = (slot_of == slot) & block_live
        row_mask = jnp.repeat(chosen, rows_per).astype(hidden.dtype)
        masked = hidden * row_mask[:, None]
        results.append(
            lax.dot_general(
                masked, grad_out, (((0,), (0,)), ((), ())), preferred_element_type=jnp.float32
            )
        )
    return jnp.stack(results)


def pick(placement, device):
    return lax.dynamic_index_in_dim(placement, device, 0, keepdims=False)


def deliver(home_slots, received, expert, wanted):
    local_slot = expert % EXP_DEV
    weight = jnp.where(wanted & (jnp.arange(EXP_DEV) == local_slot), 1.0, 0.0).astype(jnp.float32)
    return home_slots + weight[:, None, None] * received[None]


def fold_replicas(home_slots, replica, placement, holder, holders):
    quarter = holders // 4
    for distance in range(1, 4):
        sender = (holder + distance * quarter) % holders
        received = from_behind(
            replica.astype(jnp.bfloat16), "expert", holders - distance * quarter
        ).astype(replica.dtype)
        expert = pick(placement, sender)
        home_slots = deliver(home_slots, received, expert, expert // EXP_DEV == holder)
    return home_slots


def body(hidden, grad_out, block_slot, block_count, replica_expert):
    holder = lax.axis_index("expert")
    holders = lax.axis_size("expert")
    gathered, peer_lists, counts = (
        lax.all_gather(hidden, "dp", axis=0, tiled=True),
        lax.all_gather(block_slot, "dp", axis=0, tiled=True),
        lax.all_gather(block_count, "dp", axis=0, tiled=True),
    )
    quarters = lax.all_to_all(grad_out, "dp", split_axis=1, concat_axis=0, tiled=True)
    slot_of = peer_lists.reshape(-1)
    places = jnp.arange(slot_of.shape[0], dtype=jnp.int32)
    block_live = places % BLOCKS < counts[places // BLOCKS]
    totals = slot_products(gathered, quarters, slot_of, block_live)
    home_slots = fold_replicas(totals[:EXP_DEV], totals[EXP_DEV], replica_expert, holder, holders)
    return home_slots.astype(jnp.bfloat16)


def solution(mesh):
    in_specs = (
        P(("dp", "expert"), None),
        P(("dp", "expert"), None),
        P(("dp", "expert"), None),
        P(("dp", "expert")),
        P(),
    )
    out_specs = P("expert", None, "dp")
    return jax.shard_map(body, mesh=mesh, in_specs=in_specs, out_specs=out_specs, check_vma=False)
```

profile of v0, /device:TPU:8, one launch (start us, length us, event | category | flops | bytes accessed | tf_op | source)
XLA Modules:
  0.0 284.3 jit_solution(3377853961594947709)
XLA Ops:
  6.5 0.0 all-gather.3.cloned.1.call-start
  6.5 0.7 all-gather.3.cloned.1.call-update
  7.3 6.4 %copy.8 = bf16[1024,2048]{0,1:T(8,128)(2,1)} copy(bf16[1024,2048]{1,0:T(8,128)(2,1)} %param.6) | data formatting | bytes 8388608 | tf_op args[1]
  13.7 0.0 copy-start.4
  13.7 0.0 copy-start.2
  13.7 0.0 copy-start.1
  13.7 5.5 %all-to-all-start = ((bf16[1024,4,512]{0,2,1:T(8,128)(2,1)}), bf16[1024,4,512]{0,2,1:T(8,128)(2,1)}, u32[]{:S(2)}, u32[]{:S(2)}) async-start(bf16[1024,4,512]{0,2,1:T(8,128)(2,1)} %bitcast.30), calls=%async_computation | async-start | bytes 8388608 | tf_op jit(solution)/shard_map/all_to_all | solution.py:62
  19.8 0.0 copy-done.4
  19.8 0.6 dynamic-slice
  20.4 0.8 dynamic-update-slice
  21.1 183.5 %all-reduce = s32[4]{0:T(128)S(1)} all-reduce(s32[4]{0:T(128)S(1)} %dynamic-update-slice), channel_id=1, replica_groups=mesh['dp'=4,'expert'=8] {'dp'}, use_global_device_ids=true, to_apply=%add | all-reduce | flops 4 | bytes 32
  204.6 0.0 copy-done.2
  204.6 11.1 %all-gather = s32[4,1,8]{2,1,0:T(1,128)S(1)} all-gather(s32[1,1,8]{2,1,0:T(1,128)S(1)} %bitcast.34), channel_id=1, replica_groups=mesh['dp'=4,'expert'=8] {'dp'}, dimensions={0}, use_global_device_ids=true | all-gather | bytes 160 | tf_op jit(solution)/shard_map/all_gather | solution.py:59
  215.8 0.0 copy-done.1
  215.8 0.7 fusion.24
  224.6 0.1 eq.71
  224.7 0.1 eq.79
  224.8 0.1 eq.73
  224.9 0.7 fusion.25
  225.6 2.6 and_convert_fusion
  228.2 0.1 broadcast_bitcast_fusion
  228.3 0.1 broadcast_bitcast_fusion.1
  228.4 0.0 all-to-all-done
  228.4 6.3 %copy.9 = bf16[4,1024,512]{2,1,0:T(8,128)(2,1)} copy(bf16[4,1024,512]{1,2,0:T(8,128)(2,1)} %bitcast.9) | data formatting | bytes 8388608 | tf_op jit(solution)/shard_map/all_to_all | solution.py:62
  234.6 0.0 all-gather.3.cloned.1.call-done
  234.6 0.0 copy-start
  234.6 0.0 copy-start.3
  234.6 7.7 %fusion.18 = bf16[768,512]{1,0:T(8,128)(2,1)S(1)} fusion(bf16[4096,512]{1,0:T(8,128)(2,1)} %bitcast.31, bf16[4096,768]{1,0:T(8,128)(2,1)} %all-gather.3.cloned.1.call-done, bf16[4096]{0:T(1024)(128)(2,1)S(1)} %broadcast_bitcast_fusion), kind=kOutput, calls=%fused_computation.15 | convolution fusion | flops 3224764416 | bytes 11280384 | tf_op jit(solution)/shard_map/dot_general | solution.py:25
  242.3 1.5 collective-permute-start.2
  243.9 1.5 collective-permute-start.1
  245.4 1.4 collective-permute-start
  246.8 0.0 copy-done
  246.8 0.0 copy-done.3
  246.8 3.6 %fusion.15 = f32[1,768,512]{2,1,0:T(8,128)S(1)} fusion(bf16[4096,512]{1,0:T(8,128)(2,1)S(1)} %bitcast.32, bf16[4096,768]{1,0:T(8,128)(2,1)S(1)} %copy-done.3, bf16[4096]{0:T(1024)(128)(2,1)S(1)} %get-tuple-element.19), kind=kOutput, calls=%fused_computation.14 | convolution fusion | flops 3224371200 | bytes 12066816 | tf_op jit(solution)/shard_map/dot_general | solution.py:25
  250.4 3.6 %fusion.12 = f32[1,768,512]{2,1,0:T(8,128)S(1)} fusion(bf16[4096,512]{1,0:T(8,128)(2,1)S(1)} %bitcast.33, bf16[4096,768]{1,0:T(8,128)(2,1)S(1)} %copy-done.3, bf16[4096]{0:T(1024)(128)(2,1)S(1)} %get-tuple-element.20), kind=kOutput, calls=%fused_computation.13 | convolution fusion | flops 3224371200 | bytes 12066816 | tf_op jit(solution)/shard_map/dot_general | solution.py:25
  254.0 9.8 %collective-permute-done.2 = bf16[768,512]{1,0:T(8,128)(2,1)S(1)} collective-permute-done((bf16[768,512]{1,0:T(8,128)(2,1)S(1)}, bf16[768,512]{1,0:T(8,128)(2,1)S(1)}, u32[]{:S(2)}, u32[]{:S(2)}) %collective-permute-start.2) | collective-permute-done | bytes 786464 | tf_op jit(solution)/shard_map/ppermute | solution.py:13
  263.8 0.2 convert_element_type.59
  264.0 10.8 %collective-permute-done.1 = bf16[768,512]{1,0:T(8,128)(2,1)S(1)} collective-permute-done((bf16[768,512]{1,0:T(8,128)(2,1)S(1)}, bf16[768,512]{1,0:T(8,128)(2,1)S(1)}, u32[]{:S(2)}, u32[]{:S(2)}) %collective-permute-start.1) | collective-permute-done | bytes 786464 | tf_op jit(solution)/shard_map/ppermute | solution.py:13
  274.8 0.2 convert_element_type.58
  275.0 0.0 collective-permute-done
  275.0 0.2 convert_element_type.57
  275.2 2.3 fusion.8
  (5 shorter events, 0.1 us)
Async XLA Ops:
  6.5 228.1 %all-gather.3.cloned.1.call-start = ((), (), s32[]{:S(2)}) async-start(), calls=%async_computation.1 | async-start | bytes 7864320 | tf_op jit(solution)/shard_map/all_gather | solution.py:58
  13.7 6.1 %copy-start.4 = (u32[32]{0:T(128)S(1)}, u32[32]{0:T(128)}, u32[]{:S(2)}) copy-start(u32[32]{0:T(128)} %constant.118) | copy-start | bytes 388
  13.7 191.0 %copy-start.2 = (s32[1,8]{1,0:T(1,128)S(1)}, s32[1,8]{1,0:T(1,128)}, u32[]{:S(2)}) copy-start(s32[1,8]{1,0:T(1,128)} %param.7) | copy-start | bytes 100
  13.7 202.1 %copy-start.1 = (s32[8]{0:T(128)S(1)}, s32[8]{0:T(128)}, u32[]{:S(2)}) copy-start(s32[8]{0:T(128)} %param.9) | copy-start | bytes 100
  13.7 214.7 %all-to-all-start = ((bf16[1024,4,512]{0,2,1:T(8,128)(2,1)}), bf16[1024,4,512]{0,2,1:T(8,128)(2,1)}, u32[]{:S(2)}, u32[]{:S(2)}) async-start(bf16[1024,4,512]{0,2,1:T(8,128)(2,1)} %bitcast.30), calls=%async_computation | async-start | bytes 8388608 | tf_op jit(solution)/shard_map/all_to_all | solution.py:62
  234.6 12.2 %copy-start = (bf16[4,1024,512]{2,1,0:T(8,128)(2,1)S(1)}, bf16[4,1024,512]{2,1,0:T(8,128)(2,1)}, u32[]{:S(2)}) copy-start(bf16[4,1024,512]{2,1,0:T(8,128)(2,1)} %copy.9) | copy-start | bytes 12582916
  234.6 12.2 %copy-start.3 = (bf16[4096,768]{1,0:T(8,128)(2,1)S(1)}, bf16[4096,768]{1,0:T(8,128)(2,1)}, u32[]{:S(2)}) copy-start(bf16[4096,768]{1,0:T(8,128)(2,1)} %all-gather.3.cloned.1.call-done) | copy-start | bytes 18874372
  242.3 21.4 %collective-permute-start.2 = (bf16[768,512]{1,0:T(8,128)(2,1)S(1)}, bf16[768,512]{1,0:T(8,128)(2,1)S(1)}, u32[]{:S(2)}, u32[]{:S(2)}) collective-permute-start(bf16[768,512]{1,0:T(8,128)(2,1)S(1)} %fusion.18), channel_id=1, source_target_pairs={{6,0},{7,1},{0,2},{1,3},{2,4},{3,5},{4,6},{5,7},{14,8},{15,9},{8,1... | collective-permute-start | bytes 2359304 | tf_op jit(solution)/shard_map/ppermute | solution.py:13
  243.9 30.9 %collective-permute-start.1 = (bf16[768,512]{1,0:T(8,128)(2,1)S(1)}, bf16[768,512]{1,0:T(8,128)(2,1)S(1)}, u32[]{:S(2)}, u32[]{:S(2)}) collective-permute-start(bf16[768,512]{1,0:T(8,128)(2,1)S(1)} %fusion.18), channel_id=1, source_target_pairs={{4,0},{5,1},{6,2},{7,3},{0,4},{1,5},{2,6},{3,7},{12,8},{13,9},{14,... | collective-permute-start | bytes 2359304 | tf_op jit(solution)/shard_map/ppermute | solution.py:13
  245.4 29.6 %collective-permute-start = (bf16[768,512]{1,0:T(8,128)(2,1)S(1)}, bf16[768,512]{1,0:T(8,128)(2,1)S(1)}, u32[]{:S(2)}, u32[]{:S(2)}) collective-permute-start(bf16[768,512]{1,0:T(8,128)(2,1)S(1)} %fusion.18), channel_id=1, source_target_pairs={{2,0},{3,1},{4,2},{5,3},{6,4},{7,5},{0,6},{1,7},{10,8},{11,9},{12,... | collective-permute-start | bytes 2359304 | tf_op jit(solution)/shard_map/ppermute | solution.py:13
Sparse Core Ops, SparseCore 0:
  8.9 201.4 all-gather.2
where the time goes:
time: 288 us; the launch traced here: 284 us
  blocking collectives  195 us (68%)
  between operations  22.3 us (8%)
  waiting for transfers between devices  21.3 us (7%)
  local copies, waits for them, and re-layouts  15.8 us (5%)
  matrix products  14.8 us (5%)
  starting transfers between devices  9.96 us (3%)
  other arithmetic  5.54 us (2%)
    unnamed x1, blocking collectives  183 us
    ppermute x3, waiting for transfers between devices, from_behind(): return lax.ppermute(block, axis, route)  20.6 us
    dot_general x3, matrix products, slot_products(): lax.dot_general(masked, grad_out, (((0,), (0,)), ((), ())), preferred_ele...  14.8 us
    all_gather x1, blocking collectives, body(): lax.all_gather(block_slot, 'dp', axis=0, tiled=True)  11.1 us
    unnamed x14, local copies, waits for them, and re-layouts  7.76 us
    all_to_all x1, local copies, waits for them, and re-layouts, body(): lax.all_to_all(grad_out, 'dp', split_axis=1, concat_axis=0, tiled=True)  6.26 us
  transfers between devices with their start and end apart: 5, of which 2 were waited for; matrix products, arithmetic and copies ran while one was open for 9% of the time, Pallas kernels for 0%

commit v1 on v0

v1 whole, which is shorter than its diff:
```python
import functools

import jax
import jax.numpy as jnp
from jax import lax
from jax.experimental import pallas as pl
from jax.experimental.pallas import tpu as pltpu
from jax.sharding import PartitionSpec as P

EXP_DEV = 2
COLD, HOT, REPLICA = 0, 1, 2


class Route:
    def __init__(self, placement, dp, expert, holders):
        quarter = holders // 4
        group, place = lax.rem(expert, quarter), lax.div(expert, quarter)

        def at(flip):
            return jnp.bitwise_xor(place, flip) * quarter + group

        self.d = dp
        self.here = expert
        self.near = {flip: at(flip) for flip in (1, 2, 3)}
        self.mine = placement[expert]
        self.theirs = {flip: placement[self.near[flip]] for flip in (1, 2, 3)}
        hot = jnp.int32(EXP_DEV - 1)
        for flip in (3, 1, 2):
            owner = self.theirs[flip]
            hot = jnp.where(self.home(owner) == expert, lax.rem(owner, EXP_DEV), hot)
        self.hot = hot
        self.at_home = self.home(self.mine) == expert

    def home(self, owner):
        return lax.div(owner, EXP_DEV)

    def kind(self, slot):
        local = jnp.where((slot == EXP_DEV) & self.at_home, lax.rem(self.mine, EXP_DEV), slot)
        return jnp.where(local == EXP_DEV, REPLICA, jnp.where(local == self.hot, HOT, COLD))

    def arrives(self, flip):
        return self.home(self.theirs[flip]) == self.here

    def passes(self, first, second):
        return self.home(self.theirs[first]) == self.near[second]

    def goes(self, flip):
        return self.home(self.mine) == self.near[flip]


def piece_kernel(jobs, holders, width, n_in, *refs):
    slots, counts, placement, hidden, grad = refs[:5]
    arrived = refs[5 : 5 + n_in]
    n_out = sum(len(job["rows"]) for job in jobs)
    outs = refs[5 + n_in : 5 + n_in + n_out]
    hidden_v, grad_v, total, sem = refs[5 + n_in + n_out :]
    blocks = slots.shape[1]
    rows = hidden.shape[0] // blocks
    route = Route(placement, lax.axis_index("dp"), lax.axis_index("expert"), holders)
    fetch = pltpu.make_async_copy(hidden, hidden_v, sem.at[0])
    fetch.start()
    columns = []
    for j, job in enumerate(jobs):
        begin = pl.multiple_of(job["column"](route.d) * width, width)
        columns.append(pltpu.make_async_copy(grad.at[:, pl.ds(begin, width)], grad_v.at[j], sem.at[1 + j]))
        columns[-1].start()
    fetch.wait()
    outs = list(outs)
    for j, job in enumerate(jobs):
        columns[j].wait()
        total[...] = jnp.zeros_like(total)

        @pl.loop(0, blocks)
        def _(b):
            @pl.when((b < counts[0]) & (route.kind(slots[0, b]) == job["kind"]))
            def _():
                at = pl.ds(pl.multiple_of(b * rows, rows), rows)
                total[...] += lax.dot_general(
                    hidden_v[at, :], grad_v[j, at, :], (((0,), (0,)), ((), ())), preferred_element_type=jnp.float32
                )

        for position, part, index, when in job["adds"]:
            chosen = arrived[position] if index is None else arrived[position].at[index]

            def add(chosen=chosen, part=part):
                total[part, :] += chosen[...].astype(jnp.float32)

            if when is None:
                add()
            else:
                pl.when(when(route))(add)
        for part in job["rows"]:
            outs.pop(0)[...] = total[part, :].astype(jnp.bfloat16)


def make_pieces(jobs, env, arrived=()):
    hidden, grad, slots, counts, placement, holders, width = env
    ff = hidden.shape[1]
    shapes = [(part.stop - part.start, width) for job in jobs for part in job["rows"]]
    smem, vmem, anywhere = (pl.BlockSpec(memory_space=space) for space in (pltpu.SMEM, pltpu.VMEM, pl.ANY))
    return pl.pallas_call(
        functools.partial(piece_kernel, jobs, holders, width, len(arrived)),
        out_shape=[jax.ShapeDtypeStruct(shape, jnp.bfloat16) for shape in shapes],
        in_specs=[smem, smem, smem, anywhere, anywhere] + [vmem] * len(arrived),
        out_specs=[vmem] * len(shapes),
        scratch_shapes=[
            pltpu.VMEM(hidden.shape, hidden.dtype),
            pltpu.VMEM((len(jobs), hidden.shape[0], width), grad.dtype),
            pltpu.VMEM((ff, width), jnp.float32),
            pltpu.SemaphoreType.DMA((1 + len(jobs),)),
        ],
        compiler_params=pltpu.CompilerParams(vmem_limit_bytes=32 << 20),
        cost_estimate=pl.CostEstimate(
            flops=len(jobs) * hidden.shape[0] * ff * width,
            bytes_accessed=2 * (hidden.size + len(jobs) * (hidden.shape[0] + ff) * width),
            transcendentals=0,
        ),
    )(slots, counts, placement, hidden, grad, *arrived)


def relay_kernel(holders, legs, placement, *refs):
    route = Route(placement, lax.axis_index("dp"), lax.axis_index("expert"), holders)
    for i, (first, second) in enumerate(legs):
        own, came, out = refs[i], refs[len(legs) + i], refs[2 * len(legs) + i]
        mine, other = route.goes(second), route.passes(first, second)
        zero = jnp.zeros(own.shape, jnp.float32)
        out[...] = (
            jnp.where(mine, own[...].astype(jnp.float32), zero) + jnp.where(other, came[...].astype(jnp.float32), zero)
        ).astype(out.dtype)


def relay(placement, holders, legs, own, came):
    smem, vmem = pl.BlockSpec(memory_space=pltpu.SMEM), pl.BlockSpec(memory_space=pltpu.VMEM)
    return pl.pallas_call(
        functools.partial(relay_kernel, holders, legs),
        out_shape=[jax.ShapeDtypeStruct(a.shape, a.dtype) for a in own],
        in_specs=[smem] + [vmem] * (2 * len(legs)),
        out_specs=[vmem] * len(legs),
        compiler_params=pltpu.CompilerParams(vmem_limit_bytes=32 << 20),
        cost_estimate=pl.CostEstimate(flops=sum(a.size for a in own), bytes_accessed=6 * sum(a.size for a in own), transcendentals=0),
    )(placement, *own, *came)


def flip_pairs(holders, flip):
    quarter = holders // 4
    return [(k, ((k // quarter) ^ flip) * quarter + k % quarter) for k in range(holders)]


def finish_kernel(hot_ref, cold, hot, out):
    at = hot_ref[0]
    out[1 - at] = cold[...]
    out[at] = hot[...]


def body(hidden, grad, slots, counts, placement):
    n, holders = lax.axis_size("dp"), lax.axis_size("expert")
    ff, width = hidden.shape[1], grad.shape[1] // n
    env = (hidden, grad, slots, counts, placement, holders, width)
    half = ff // 2
    whole, halves = slice(0, ff), (slice(0, half), slice(half, ff))
    legs = ((1, 2), (2, 1))

    def right_column(t):
        return lambda d: jnp.clip(n - t + d, 0, n - 1)

    def left_column(t):
        return lambda d: jnp.clip(t - n + d, 0, n - 1)

    def round_job(mask):
        return {"kind": REPLICA, "column": lambda d: jnp.bitwise_xor(d, mask), "rows": halves, "adds": []}

    def first_job(kind, adds=()):
        return {"kind": kind, "column": lambda d: jnp.where(d == 0, n - 1, 0), "rows": (whole,), "adds": list(adds)}

    def hop(x, flip):
        return lax.ppermute(x, "expert", flip_pairs(holders, flip))

    def swap(own):
        came = [hop(a, first) for a, (first, _) in zip(own, legs)]
        relayed = relay(placement, holders, legs, own, came)
        second = [hop(a, second) for a, (_, second) in zip(relayed, legs)]
        return list(came) + list(second)

    def plane_adds(base, columns, masks):
        adds = []
        for i, mask in enumerate(masks):
            for leg, (first, second) in enumerate(legs):
                here = lambda r, mask=mask: jnp.bitwise_xor(r.d, mask) == columns(r.d)
                adds.append((base + 4 * i + leg, halves[leg], None, lambda r, h=here, f=first: h(r) & r.arrives(f)))
                adds.append((base + 4 * i + 2 + leg, halves[leg], None, here))
        return adds

    def step_masks(t):
        right = sorted({(n - t + d) ^ d for d in range(t)})
        left = sorted({(t - n + d) ^ d for d in range(n - t, n)})
        return right, left

    def send(x, pairs):
        return lax.ppermute(x, "dp", pairs)

    def right_pairs(t):
        return [(d, d + 1) for d in range(t)]

    def left_pairs(t):
        return [(n - 1 - d, n - 2 - d) for d in range(t)]

    def step(kind, t, came_right, came_left, planes):
        right, left = step_masks(t)
        arrived = [came_right] + ([came_left] if came_left is not came_right else [])
        r_adds, l_adds = [(0, whole, None, None)], [(len(arrived) - 1, whole, None, None)]
        if planes is not None:
            masks = sorted(set(right) | set(left))
            base = len(arrived)
            arrived = arrived + [a for mask in masks for a in planes[mask]]
            r_adds += [x for x in plane_adds(base, right_column(t), masks)]
            l_adds += [x for x in plane_adds(base, left_column(t), masks)]
        jobs = [
            {"kind": kind, "column": right_column(t), "rows": (whole,), "adds": r_adds},
            {"kind": kind, "column": left_column(t), "rows": (whole,), "adds": l_adds},
        ]
        r, l = make_pieces(jobs, env, arrived)
        return send(r, right_pairs(t)), send(l, left_pairs(t))

    def last(kind, came_right, came_left, planes):
        adds, arrived = [(0, whole, None, None), (1, whole, None, None)], [came_right, came_left]
        if planes is not None:
            adds += plane_adds(2, lambda d: d, [0])
            arrived = arrived + list(planes[0])
        job = {"kind": kind, "column": lambda d: d, "rows": (whole,), "adds": adds}
        return make_pieces([job], env, arrived)[0]

    planes = {}
    first_pairs = [(0, 1), (n - 1, n - 2)]
    cold_1, *own = make_pieces([first_job(COLD), round_job(n - 1)], env)
    cold_r = cold_l = send(cold_1, first_pairs)
    planes[n - 1] = swap(own)
    for mask in range(n - 2, -1, -1):
        planes[mask] = swap(make_pieces([round_job(mask)], env))
    hot_adds = plane_adds(0, lambda d: jnp.where(d == 0, n - 1, 0), [n - 1])
    (hot_1,) = make_pieces([first_job(HOT, hot_adds)], env, planes[n - 1])
    hot_r = hot_l = send(hot_1, first_pairs)
    for t in range(2, n):
        cold_r, cold_l = step(COLD, t, cold_r, cold_l, None)
        hot_r, hot_l = step(HOT, t, hot_r, hot_l, planes)
    cold = last(COLD, cold_r, cold_l, None)
    hot = last(HOT, hot_r, hot_l, planes)
    route = Route(placement, lax.axis_index("dp"), lax.axis_index("expert"), holders)
    first = jnp.where(route.hot == 0, hot, cold)
    second = jnp.where(route.hot == 0, cold, hot)
    return jnp.stack([first, second])


def solution(mesh):
    in_specs = (
        P(("dp", "expert"), None),
        P(("dp", "expert"), None),
        P(("dp", "expert"), None),
        P(("dp", "expert")),
        P(),
    )
    out_specs = P("expert", None, "dp")
    return jax.shard_map(body, mesh=mesh, in_specs=in_specs, out_specs=out_specs, check_vma=False)
```

time: 288 us -> 133 us (0.46)
  blocking collectives: 195 us -> 0 us
  starting transfers between devices: 9.96 us -> 44.7 us
  Pallas kernels: 0 us -> 30.1 us
  waiting for transfers between devices: 21.3 us -> 41.1 us
  between operations: 22.3 us -> 6.4 us
  matrix products: 14.8 us -> 0 us
  local copies, waits for them, and re-layouts: 15.8 us -> 7.72 us
  other arithmetic: 5.54 us -> 1.39 us
    unnamed x1 -> x0, blocking collectives: 183 us -> none
    ppermute x3 -> x26, starting transfers between devices: 4.5 us -> 44.7 us  [the longest x10 26.4 us: send(): return lax.ppermute(x, 'dp', pairs)]
    pallas_call x0 -> x15, Pallas kernels: none -> 30.1 us  [the longest x11 25.9 us: make_pieces(): pl.pallas_call(functools.partial(piece_kernel, jobs, holders, width, len(...]
    ppermute x3 -> x26, waiting for transfers between devices: 20.6 us -> 41.1 us  [the longest x16 21.8 us: hop(): return lax.ppermute(x, 'expert', flip_pairs(holders, flip))]
    dot_general x3 -> x0, matrix products: 14.8 us -> none  [slot_products(): lax.dot_general(masked, grad_out, (((0,), (0,)), ((), ())), preferred_ele...]
    all_gather x1 -> x0, blocking collectives: 11.1 us -> none  [body(): lax.all_gather(block_slot, 'dp', axis=0, tiled=True)]
    all_to_all x1 -> x0, local copies, waits for them, and re-layouts: 6.26 us -> none  [body(): lax.all_to_all(grad_out, 'dp', split_axis=1, concat_axis=0, tiled=True)]
    convert_element_type x6 -> x0, other arithmetic: 5.5 us -> none  [the longest x2 2.61 us: slot_products(): row_mask = jnp.repeat(chosen, rows_per).astype(hidden.dtype)]
  transfers between devices with their start and end apart: 5 -> 26, of which waited for: 2 -> 13; matrix products, arithmetic and copies ran while one was open for 9% -> 0% of each run, Pallas kernels for 0% -> 19%
where the time goes in v1:
time: 133 us; the launch traced here: 131 us
  starting transfers between devices  44.7 us (34%)
  waiting for transfers between devices  41.1 us (31%)
  Pallas kernels  30.1 us (23%)
  local copies, waits for them, and re-layouts  7.72 us (6%)
  between operations  6.4 us (5%)
  other arithmetic  1.39 us (1%)
    ppermute x10, starting transfers between devices, send(): return lax.ppermute(x, 'dp', pairs)  26.4 us
    pallas_call x11, Pallas kernels, make_pieces(): pl.pallas_call(functools.partial(piece_kernel, jobs, holders, width, len(...  25.9 us
    ppermute x16, waiting for transfers between devices, hop(): return lax.ppermute(x, 'expert', flip_pairs(holders, flip))  21.8 us
    ppermute x10, waiting for transfers between devices, send(): return lax.ppermute(x, 'dp', pairs)  19.3 us
    ppermute x16, starting transfers between devices, hop(): return lax.ppermute(x, 'expert', flip_pairs(holders, flip))  18.4 us
    unnamed x18, local copies, waits for them, and re-layouts  7.11 us
    pallas_call x4, Pallas kernels, relay(): pl.pallas_call(functools.partial(relay_kernel, holders, legs), out_shape=...  4.16 us
  transfers between devices with their start and end apart: 26, of which 13 were waited for; matrix products, arithmetic and copies ran while one was open for 0% of the time, Pallas kernels for 19%

profile of v1, /device:TPU:8, one launch (start us, length us, event | category | flops | bytes accessed | tf_op | source)
XLA Modules:
  0.0 131.4 jit_solution(10011999045305212291)
XLA Ops:
  0.7 2.2 %copy-done = bf16[1024,2048]{1,0:T(8,128)(2,1)S(1)} copy-done((bf16[1024,2048]{1,0:T(8,128)(2,1)S(1)}, bf16[1024,2048]{1,0:T(8,128)(2,1)}, u32[]{:S(2)}) %copy-start) | copy-done | bytes 4194328
  2.8 1.4 %copy-done.3 = bf16[1024,768]{1,0:T(8,128)(2,1)S(1)} copy-done((bf16[1024,768]{1,0:T(8,128)(2,1)S(1)}, bf16[1024,768]{1,0:T(8,128)(2,1)}, u32[]{:S(2)}) %copy-start.3) | copy-done | bytes 1572888
  5.6 2.4 %shard_map.55 = (bf16[768,512]{1,0:T(8,128)(2,1)S(1)}, bf16[384,512]{1,0:T(8,128)(2,1)S(1)}, bf16[384,512]{1,0:T(8,128)(2,1)S(1)}) custom-call(s32[1,8]{1,0:T(1,128)S(1)} %copy-done.7, s32[1]{0:T(128)S(6)} %copy.6.refs_1_, s32[8]{0:T(128)S(1)} %copy-done.5, bf16[1024,768]{1,0:T(8,128)(2,1)S(1)} %copy-done.3, bf16[1024,2048]{1,0:T(8,128)(2,1)S(1)} %copy-done), custom_call_target="tpu_custom_call" | custom-call | flops 805306368 | bytes 5242880 | tf_op jit(solution)/shard_map/pallas_call | solution.py:101
  8.0 1.6 %collective-permute-start = (bf16[384,512]{1,0:T(8,128)(2,1)S(1)}, bf16[384,512]{1,0:T(8,128)(2,1)S(1)}, u32[]{:S(2)}, u32[]{:S(2)}) collective-permute-start(bf16[384,512]{1,0:T(8,128)(2,1)S(1)} %get-tuple-element.30.refs_0_), channel_id=1, source_target_pairs={{0,2},{1,3},{2,0},{3,1},{4,6},{5,7},{6,4},{7,5},{8,10},{9,11},{10,... | collective-permute-start | bytes 1179656 | tf_op jit(solution)/shard_map/ppermute | solution.py:176
  9.6 2.3 %collective-permute-start.1 = (bf16[384,512]{1,0:T(8,128)(2,1)S(1)}, bf16[384,512]{1,0:T(8,128)(2,1)S(1)}, u32[]{:S(2)}, u32[]{:S(2)}) collective-permute-start(bf16[384,512]{1,0:T(8,128)(2,1)S(1)} %get-tuple-element.31.refs_1_), channel_id=1, source_target_pairs={{0,4},{1,5},{2,6},{3,7},{4,0},{5,1},{6,2},{7,3},{8,12},{9,13},{10,... | collective-permute-start | bytes 1179656 | tf_op jit(solution)/shard_map/ppermute | solution.py:176
  11.9 1.3 collective-permute-start.21
  13.2 6.6 %collective-permute-done.refs_2_.refs_5_.refs_11_ = bf16[384,512]{1,0:T(8,128)(2,1)S(1)} collective-permute-done((bf16[384,512]{1,0:T(8,128)(2,1)S(1)}, bf16[384,512]{1,0:T(8,128)(2,1)S(1)}, u32[]{:S(2)}, u32[]{:S(2)}) %collective-permute-start) | collective-permute-done | bytes 393248 | tf_op jit(solution)/shard_map/ppermute | solution.py:176
  19.7 1.7 %collective-permute-done.1.refs_3_.refs_6_.refs_12_ = bf16[384,512]{1,0:T(8,128)(2,1)S(1)} collective-permute-done((bf16[384,512]{1,0:T(8,128)(2,1)S(1)}, bf16[384,512]{1,0:T(8,128)(2,1)S(1)}, u32[]{:S(2)}, u32[]{:S(2)}) %collective-permute-start.1) | collective-permute-done | bytes 393248 | tf_op jit(solution)/shard_map/ppermute | solution.py:176
  22.3 1.8 %collective-permute-start.2 = (bf16[384,512]{1,0:T(8,128)(2,1)S(1)}, bf16[384,512]{1,0:T(8,128)(2,1)S(1)}, u32[]{:S(2)}, u32[]{:S(2)}) collective-permute-start(bf16[384,512]{1,0:T(8,128)(2,1)S(1)} %get-tuple-element.32), channel_id=1, source_target_pairs={{0,4},{1,5},{2,6},{3,7},{4,0},{5,1},{6,2},{7,3},{8,12},{9,13},{10,... | collective-permute-start | bytes 1179656 | tf_op jit(solution)/shard_map/ppermute | solution.py:176
  24.5 1.6 %shard_map.58 = (bf16[384,512]{1,0:T(8,128)(2,1)S(1)}, bf16[384,512]{1,0:T(8,128)(2,1)S(1)}) custom-call(s32[1,8]{1,0:T(1,128)S(1)} %copy-done.7, s32[1]{0:T(128)S(6)} %copy.6.refs_1_, s32[8]{0:T(128)S(1)} %copy-done.5, bf16[1024,768]{1,0:T(8,128)(2,1)S(1)} %copy-done.4, bf16[1024,2048]{1,0:T(8,128)(2,1)S(1)} %copy-done.1), custom_call_target="tpu_custom_call" | custom-call | flops 402653184 | bytes 3407872 | tf_op jit(solution)/shard_map/pallas_call | solution.py:101
  26.0 2.1 %collective-permute-start.5 = (bf16[384,512]{1,0:T(8,128)(2,1)S(1)}, bf16[384,512]{1,0:T(8,128)(2,1)S(1)}, u32[]{:S(2)}, u32[]{:S(2)}) collective-permute-start(bf16[384,512]{1,0:T(8,128)(2,1)S(1)} %get-tuple-element.34.refs_0_), channel_id=1, source_target_pairs={{0,2},{1,3},{2,0},{3,1},{4,6},{5,7},{6,4},{7,5},{8,10},{9,11},{10,... | collective-permute-start | bytes 1179656 | tf_op jit(solution)/shard_map/ppermute | solution.py:176
  28.4 5.9 %collective-permute-done.2.refs_7_.refs_13_ = bf16[384,512]{1,0:T(8,128)(2,1)S(1)} collective-permute-done((bf16[384,512]{1,0:T(8,128)(2,1)S(1)}, bf16[384,512]{1,0:T(8,128)(2,1)S(1)}, u32[]{:S(2)}, u32[]{:S(2)}) %collective-permute-start.2) | collective-permute-done | bytes 393248 | tf_op jit(solution)/shard_map/ppermute | solution.py:176
  34.4 1.8 %collective-permute-done.3.refs_8_.refs_14_ = bf16[384,512]{1,0:T(8,128)(2,1)S(1)} collective-permute-done((bf16[384,512]{1,0:T(8,128)(2,1)S(1)}, bf16[384,512]{1,0:T(8,128)(2,1)S(1)}, u32[]{:S(2)}, u32[]{:S(2)}) %collective-permute-start.3) | collective-permute-done | bytes 393248 | tf_op jit(solution)/shard_map/ppermute | solution.py:176
  36.2 1.2 shard_map.57
  37.4 1.3 collective-permute-start.4
  38.7 4.1 %collective-permute-done.5.refs_2_.refs_6_ = bf16[384,512]{1,0:T(8,128)(2,1)S(1)} collective-permute-done((bf16[384,512]{1,0:T(8,128)(2,1)S(1)}, bf16[384,512]{1,0:T(8,128)(2,1)S(1)}, u32[]{:S(2)}, u32[]{:S(2)}) %collective-permute-start.5) | collective-permute-done | bytes 393248 | tf_op jit(solution)/shard_map/ppermute | solution.py:176
  44.6 2.9 %shard_map.67 = (bf16[768,512]{1,0:T(8,128)(2,1)S(1)}, bf16[768,512]{1,0:T(8,128)(2,1)S(1)}) custom-call(s32[1,8]{1,0:T(1,128)S(1)} %copy-done.7, s32[1]{0:T(128)S(6)} %copy.6.refs_1_, s32[8]{0:T(128)S(1)} %copy-done.5, bf16[1024,768]{1,0:T(8,128)(2,1)S(1)} %copy-done.4, bf16[1024,2048]{1,0:T(8,128)(2,1)S(1)} %copy-done.1, ...), custom_call_target="tpu_custom_call" | custom-call | flops 805306368 | bytes 5242880 | tf_op jit(solution)/shard_map/pallas_call | solution.py:101
  47.5 5.5 %collective-permute-start.22 = (bf16[768,512]{1,0:T(8,128)(2,1)S(1)}, bf16[768,512]{1,0:T(8,128)(2,1)S(1)}, u32[]{:S(2)}, u32[]{:S(2)}) collective-permute-start(bf16[768,512]{1,0:T(8,128)(2,1)S(1)} %get-tuple-element.51), channel_id=1, source_target_pairs={{0,8},{8,16},{1,9},{9,17},{2,10},{10,18},{3,11},{11,19},{4,12},{12... | collective-permute-start | bytes 2359304 | tf_op jit(solution)/shard_map/ppermute | solution.py:199
  53.0 1.6 %shard_map.61 = (bf16[384,512]{1,0:T(8,128)(2,1)S(1)}, bf16[384,512]{1,0:T(8,128)(2,1)S(1)}) custom-call(s32[1,8]{1,0:T(1,128)S(1)} %copy-done.7, s32[1]{0:T(128)S(6)} %copy.6.refs_1_, s32[8]{0:T(128)S(1)} %copy-done.5, bf16[1024,768]{1,0:T(8,128)(2,1)S(1)} %copy-done.4, bf16[1024,2048]{1,0:T(8,128)(2,1)S(1)} %copy-done.1), custom_call_target="tpu_custom_call" | custom-call | flops 402653184 | bytes 3407872 | tf_op jit(solution)/shard_map/pallas_call | solution.py:101
  54.7 1.3 collective-permute-start.23
  56.0 1.0 collective-permute-start.12
  56.9 2.8 %collective-permute-done.4.refs_5_ = bf16[768,512]{1,0:T(8,128)(2,1)S(1)} collective-permute-done((bf16[768,512]{1,0:T(8,128)(2,1)S(1)}, bf16[768,512]{1,0:T(8,128)(2,1)S(1)}, u32[]{:S(2)}, u32[]{:S(2)}) %collective-permute-start.4) | collective-permute-done | bytes 786464 | tf_op jit(solution)/shard_map/ppermute | solution.py:199
  59.7 2.3 %shard_map.60 = (bf16[768,512]{1,0:T(8,128)(2,1)S(1)}, bf16[768,512]{1,0:T(8,128)(2,1)S(1)}) custom-call(s32[1,8]{1,0:T(1,128)S(1)} %copy-done.7, s32[1]{0:T(128)S(6)} %copy.6.refs_1_, s32[8]{0:T(128)S(1)} %copy-done.5, bf16[1024,768]{1,0:T(8,128)(2,1)S(1)} %copy-done.4, bf16[1024,2048]{1,0:T(8,128)(2,1)S(1)} %copy-done.1, ...), custom_call_target="tpu_custom_call" | custom-call | flops 805306368 | bytes 5242880 | tf_op jit(solution)/shard_map/pallas_call | solution.py:101
  62.0 1.3 collective-permute-start.10
  63.3 4.6 %collective-permute-start.9 = (bf16[768,512]{1,0:T(8,128)(2,1)S(1)}, bf16[768,512]{1,0:T(8,128)(2,1)S(1)}, u32[]{:S(2)}, u32[]{:S(2)}) collective-permute-start(bf16[768,512]{1,0:T(8,128)(2,1)S(1)} %get-tuple-element.38), channel_id=1, source_target_pairs={{0,8},{8,16},{1,9},{9,17},{2,10},{10,18},{3,11},{11,19},{4,12},{12... | collective-permute-start | bytes 2359304 | tf_op jit(solution)/shard_map/ppermute | solution.py:199
  67.9 0.8 shard_map.62
  68.8 2.6 %collective-permute-start.13 = (bf16[384,512]{1,0:T(8,128)(2,1)S(1)}, bf16[384,512]{1,0:T(8,128)(2,1)S(1)}, u32[]{:S(2)}, u32[]{:S(2)}) collective-permute-start(bf16[384,512]{1,0:T(8,128)(2,1)S(1)} %get-tuple-element.42), channel_id=1, source_target_pairs={{0,4},{1,5},{2,6},{3,7},{4,0},{5,1},{6,2},{7,3},{8,12},{9,13},{10,... | collective-permute-start | bytes 1179656 | tf_op jit(solution)/shard_map/ppermute | solution.py:176
  71.4 5.2 %collective-permute-done.22.refs_5_ = bf16[768,512]{1,0:T(8,128)(2,1)S(1)} collective-permute-done((bf16[768,512]{1,0:T(8,128)(2,1)S(1)}, bf16[768,512]{1,0:T(8,128)(2,1)S(1)}, u32[]{:S(2)}, u32[]{:S(2)}) %collective-permute-start.22) | collective-permute-done | bytes 786464 | tf_op jit(solution)/shard_map/ppermute | solution.py:199
  77.1 1.6 %shard_map.64 = (bf16[384,512]{1,0:T(8,128)(2,1)S(1)}, bf16[384,512]{1,0:T(8,128)(2,1)S(1)}) custom-call(s32[1,8]{1,0:T(1,128)S(1)} %copy-done.7, s32[1]{0:T(128)S(6)} %copy.6.refs_1_, s32[8]{0:T(128)S(1)} %copy-done.5, bf16[1024,768]{1,0:T(8,128)(2,1)S(1)} %copy-done.4, bf16[1024,2048]{1,0:T(8,128)(2,1)S(1)} %copy-done.1), custom_call_target="tpu_custom_call" | custom-call | flops 402653184 | bytes 3407872 | tf_op jit(solution)/shard_map/pallas_call | solution.py:101
  78.7 3.8 %shard_map.68 = (bf16[768,512]{1,0:T(8,128)(2,1)S(1)}, bf16[768,512]{1,0:T(8,128)(2,1)}) custom-call(s32[1,8]{1,0:T(1,128)S(1)} %copy-done.7, s32[1]{0:T(128)S(6)} %copy.6.refs_1_, s32[8]{0:T(128)S(1)} %copy-done.5, bf16[1024,768]{1,0:T(8,128)(2,1)S(1)} %copy-done.4, bf16[1024,2048]{1,0:T(8,128)(2,1)S(1)} %copy-done.1, ...), custom_call_target="tpu_custom_call" | custom-call | flops 805306368 | bytes 5242880 | tf_op jit(solution)/shard_map/pallas_call | solution.py:101
  82.5 2.1 %collective-permute-start.24 = (bf16[768,512]{1,0:T(8,128)(2,1)S(1)}, bf16[768,512]{1,0:T(8,128)(2,1)S(1)}, u32[]{:S(2)}, u32[]{:S(2)}) collective-permute-start(bf16[768,512]{1,0:T(8,128)(2,1)S(1)} %get-tuple-element.53), channel_id=1, source_target_pairs={{0,8},{8,16},{16,24},{1,9},{9,17},{17,25},{2,10},{10,18},{18,26},{... | collective-permute-start | bytes 2359304 | tf_op jit(solution)/shard_map/ppermute | solution.py:199
  84.6 1.2 collective-permute-start.17
  85.8 1.7 %collective-permute-done.14.refs_10_ = bf16[384,512]{1,0:T(8,128)(2,1)S(1)} collective-permute-done((bf16[384,512]{1,0:T(8,128)(2,1)S(1)}, bf16[384,512]{1,0:T(8,128)(2,1)S(1)}, u32[]{:S(2)}, u32[]{:S(2)}) %collective-permute-start.14) | collective-permute-done | bytes 393248 | tf_op jit(solution)/shard_map/ppermute | solution.py:176
  87.4 0.9 collective-permute-start.18
  88.3 3.0 %collective-permute-done.10.refs_6_ = bf16[768,512]{1,0:T(8,128)(2,1)S(1)} collective-permute-done((bf16[768,512]{1,0:T(8,128)(2,1)S(1)}, bf16[768,512]{1,0:T(8,128)(2,1)S(1)}, u32[]{:S(2)}, u32[]{:S(2)}) %collective-permute-start.10) | collective-permute-done | bytes 786464 | tf_op jit(solution)/shard_map/ppermute | solution.py:199
  91.3 1.9 %collective-permute-start.25 = (bf16[768,512]{1,0:T(8,128)(2,1)}, bf16[768,512]{1,0:T(8,128)(2,1)}, u32[]{:S(2)}, u32[]{:S(2)}) collective-permute-start(bf16[768,512]{1,0:T(8,128)(2,1)} %get-tuple-element.54), channel_id=1, source_target_pairs={{24,16},{16,8},{8,0},{25,17},{17,9},{9,1},{26,18},{18,10},{10,2},{... | collective-permute-start | bytes 2359304 | tf_op jit(solution)/shard_map/ppermute | solution.py:199
  93.5 3.5 %shard_map.63 = (bf16[768,512]{1,0:T(8,128)(2,1)}, bf16[768,512]{1,0:T(8,128)(2,1)}) custom-call(s32[1,8]{1,0:T(1,128)S(1)} %copy-done.7, s32[1]{0:T(128)S(6)} %copy.6.refs_1_, s32[8]{0:T(128)S(1)} %copy-done.5, bf16[1024,768]{1,0:T(8,128)(2,1)S(1)} %copy-done.4, bf16[1024,2048]{1,0:T(8,128)(2,1)S(1)} %copy-done.1, ...), custom_call_target="tpu_custom_call" | custom-call | flops 805306368 | bytes 5242880 | tf_op jit(solution)/shard_map/pallas_call | solution.py:101
  97.0 5.3 %collective-permute-start.15 = (bf16[768,512]{1,0:T(8,128)(2,1)}, bf16[768,512]{1,0:T(8,128)(2,1)}, u32[]{:S(2)}, u32[]{:S(2)}) collective-permute-start(bf16[768,512]{1,0:T(8,128)(2,1)} %get-tuple-element.44), channel_id=1, source_target_pairs={{0,8},{8,16},{16,24},{1,9},{9,17},{17,25},{2,10},{10,18},{18,26},{... | collective-permute-start | bytes 2359304 | tf_op jit(solution)/shard_map/ppermute | solution.py:199
  102.3 1.9 %collective-permute-start.16 = (bf16[768,512]{1,0:T(8,128)(2,1)}, bf16[768,512]{1,0:T(8,128)(2,1)}, u32[]{:S(2)}, u32[]{:S(2)}) collective-permute-start(bf16[768,512]{1,0:T(8,128)(2,1)} %get-tuple-element.45), channel_id=1, source_target_pairs={{24,16},{16,8},{8,0},{25,17},{17,9},{9,1},{26,18},{18,10},{10,2},{... | collective-permute-start | bytes 2359304 | tf_op jit(solution)/shard_map/ppermute | solution.py:199
  104.2 1.6 %shard_map.65 = (bf16[384,512]{1,0:T(8,128)(2,1)}, bf16[384,512]{1,0:T(8,128)(2,1)}) custom-call(s32[8]{0:T(128)S(1)} %copy-done.5, bf16[384,512]{1,0:T(8,128)(2,1)S(1)} %get-tuple-element.46.refs_0_, bf16[384,512]{1,0:T(8,128)(2,1)S(1)} %get-tuple-element.47.refs_1_, bf16[384,512]{1,0:T(8,128)(2,1)S(1)} %collective-permute-done.17.refs_2_.refs_7_, ...), custom_call_target="tpu_custom_call" | custom-call | flops 393216 | bytes 2359296 | tf_op jit(solution)/shard_map/pallas_call | solution.py:134
  105.9 2.1 %collective-permute-start.19 = (bf16[384,512]{1,0:T(8,128)(2,1)}, bf16[384,512]{1,0:T(8,128)(2,1)S(1)}, u32[]{:S(2)}, u32[]{:S(2)}) collective-permute-start(bf16[384,512]{1,0:T(8,128)(2,1)} %get-tuple-element.48), channel_id=1, source_target_pairs={{0,4},{1,5},{2,6},{3,7},{4,0},{5,1},{6,2},{7,3},{8,12},{9,13},{10,... | collective-permute-start | bytes 1179656 | tf_op jit(solution)/shard_map/ppermute | solution.py:176
  108.0 2.3 %collective-permute-done.24.refs_5_ = bf16[768,512]{1,0:T(8,128)(2,1)S(1)} collective-permute-done((bf16[768,512]{1,0:T(8,128)(2,1)S(1)}, bf16[768,512]{1,0:T(8,128)(2,1)S(1)}, u32[]{:S(2)}, u32[]{:S(2)}) %collective-permute-start.24) | collective-permute-done | bytes 786464 | tf_op jit(solution)/shard_map/ppermute | solution.py:199
  116.9 2.2 %copy-done.2 = bf16[1024,2048]{1,0:T(8,128)(2,1)S(1)} copy-done((bf16[1024,2048]{1,0:T(8,128)(2,1)S(1)}, bf16[1024,2048]{1,0:T(8,128)(2,1)}, u32[]{:S(2)}) %copy-start.2) | copy-done | bytes 4194328
  119.1 2.5 %shard_map.69 = bf16[768,512]{1,0:T(8,128)(2,1)S(1)} custom-call(s32[1,8]{1,0:T(1,128)S(1)} %copy-done.8, s32[1]{0:T(128)S(6)} %copy.6.refs_1_, s32[8]{0:T(128)S(1)} %copy-done.6, bf16[1024,768]{1,0:T(8,128)(2,1)S(1)} %copy-done.4, bf16[1024,2048]{1,0:T(8,128)(2,1)S(1)} %copy-done.2, bf16[768,512]{1,0:T(8,128)(2,1)S(1)} %collective-permute-done.24.refs_5_, ...), custom_call_target="tpu_custom_call" | custom-call | flops 402653184 | bytes 3407872 | tf_op jit(solution)/shard_map/pallas_call | solution.py:101
  121.6 1.5 %collective-permute-done.15.refs_5_ = bf16[768,512]{1,0:T(8,128)(2,1)} collective-permute-done((bf16[768,512]{1,0:T(8,128)(2,1)}, bf16[768,512]{1,0:T(8,128)(2,1)}, u32[]{:S(2)}, u32[]{:S(2)}) %collective-permute-start.15) | collective-permute-done | bytes 786464 | tf_op jit(solution)/shard_map/ppermute | solution.py:199
  123.1 4.3 %collective-permute-done.16.refs_6_ = bf16[768,512]{1,0:T(8,128)(2,1)} collective-permute-done((bf16[768,512]{1,0:T(8,128)(2,1)}, bf16[768,512]{1,0:T(8,128)(2,1)}, u32[]{:S(2)}, u32[]{:S(2)}) %collective-permute-start.16) | collective-permute-done | bytes 786464 | tf_op jit(solution)/shard_map/ppermute | solution.py:199
  127.4 2.6 %shard_map.66 = bf16[768,512]{1,0:T(8,128)(2,1)S(1)} custom-call(s32[1,8]{1,0:T(1,128)S(1)} %copy-done.8, s32[1]{0:T(128)S(6)} %copy.6.refs_1_, s32[8]{0:T(128)S(1)} %copy-done.6, bf16[1024,768]{1,0:T(8,128)(2,1)S(1)} %copy-done.4, bf16[1024,2048]{1,0:T(8,128)(2,1)S(1)} %copy-done.2, bf16[768,512]{1,0:T(8,128)(2,1)} %collective-permute-done.15.refs_5_, ...), custom_call_target="tpu_custom_call" | custom-call | flops 402653184 | bytes 3407872 | tf_op jit(solution)/shard_map/pallas_call | solution.py:101
  130.1 1.3 pad_maximum_fusion
  (40 shorter events, 6.8 us)
Async XLA Ops:
  0.7 2.2 %copy-start = (bf16[1024,2048]{1,0:T(8,128)(2,1)S(1)}, bf16[1024,2048]{1,0:T(8,128)(2,1)}, u32[]{:S(2)}) copy-start(bf16[1024,2048]{1,0:T(8,128)(2,1)} %refs_4_.21) | copy-start | bytes 12582916
  2.8 1.4 %copy-start.3 = (bf16[1024,768]{1,0:T(8,128)(2,1)S(1)}, bf16[1024,768]{1,0:T(8,128)(2,1)}, u32[]{:S(2)}) copy-start(bf16[1024,768]{1,0:T(8,128)(2,1)} %refs_3_.21) | copy-start | bytes 4718596
  4.3 0.7 copy-start.5
  4.9 0.7 copy-start.7
  5.6 18.9 %copy-start.1 = (bf16[1024,2048]{1,0:T(8,128)(2,1)S(1)}, bf16[1024,2048]{1,0:T(8,128)(2,1)}, u32[]{:S(2)}) copy-start(bf16[1024,2048]{1,0:T(8,128)(2,1)} %refs_4_.21) | copy-start | bytes 12582916
  8.0 16.4 %copy-start.4 = (bf16[1024,768]{1,0:T(8,128)(2,1)S(1)}, bf16[1024,768]{1,0:T(8,128)(2,1)}, u32[]{:S(2)}) copy-start(bf16[1024,768]{1,0:T(8,128)(2,1)} %refs_3_.21) | copy-start | bytes 4718596
  8.0 11.7 %collective-permute-start = (bf16[384,512]{1,0:T(8,128)(2,1)S(1)}, bf16[384,512]{1,0:T(8,128)(2,1)S(1)}, u32[]{:S(2)}, u32[]{:S(2)}) collective-permute-start(bf16[384,512]{1,0:T(8,128)(2,1)S(1)} %get-tuple-element.30.refs_0_), channel_id=1, source_target_pairs={{0,2},{1,3},{2,0},{3,1},{4,6},{5,7},{6,4},{7,5},{8,10},{9,11},{10,... | collective-permute-start | bytes 1179656 | tf_op jit(solution)/shard_map/ppermute | solution.py:176
  9.6 11.9 %collective-permute-start.1 = (bf16[384,512]{1,0:T(8,128)(2,1)S(1)}, bf16[384,512]{1,0:T(8,128)(2,1)S(1)}, u32[]{:S(2)}, u32[]{:S(2)}) collective-permute-start(bf16[384,512]{1,0:T(8,128)(2,1)S(1)} %get-tuple-element.31.refs_1_), channel_id=1, source_target_pairs={{0,4},{1,5},{2,6},{3,7},{4,0},{5,1},{6,2},{7,3},{8,12},{9,13},{10,... | collective-permute-start | bytes 1179656 | tf_op jit(solution)/shard_map/ppermute | solution.py:176
  11.9 32.8 %collective-permute-start.21 = (bf16[768,512]{1,0:T(8,128)(2,1)S(1)}, bf16[768,512]{1,0:T(8,128)(2,1)S(1)}, u32[]{:S(2)}, u32[]{:S(2)}) collective-permute-start(bf16[768,512]{1,0:T(8,128)(2,1)S(1)} %get-tuple-element.50), channel_id=1, source_target_pairs={{0,8},{24,16},{1,9},{25,17},{2,10},{26,18},{3,11},{27,19},{4,12},{... | collective-permute-start | bytes 2359304 | tf_op jit(solution)/shard_map/ppermute | solution.py:199
  22.3 12.1 %collective-permute-start.2 = (bf16[384,512]{1,0:T(8,128)(2,1)S(1)}, bf16[384,512]{1,0:T(8,128)(2,1)S(1)}, u32[]{:S(2)}, u32[]{:S(2)}) collective-permute-start(bf16[384,512]{1,0:T(8,128)(2,1)S(1)} %get-tuple-element.32), channel_id=1, source_target_pairs={{0,4},{1,5},{2,6},{3,7},{4,0},{5,1},{6,2},{7,3},{8,12},{9,13},{10,... | collective-permute-start | bytes 1179656 | tf_op jit(solution)/shard_map/ppermute | solution.py:176
  24.1 12.1 %collective-permute-start.3 = (bf16[384,512]{1,0:T(8,128)(2,1)S(1)}, bf16[384,512]{1,0:T(8,128)(2,1)S(1)}, u32[]{:S(2)}, u32[]{:S(2)}) collective-permute-start(bf16[384,512]{1,0:T(8,128)(2,1)S(1)} %get-tuple-element.33), channel_id=1, source_target_pairs={{0,2},{1,3},{2,0},{3,1},{4,6},{5,7},{6,4},{7,5},{8,10},{9,11},{10,... | collective-permute-start | bytes 1179656 | tf_op jit(solution)/shard_map/ppermute | solution.py:176
  26.0 16.7 %collective-permute-start.5 = (bf16[384,512]{1,0:T(8,128)(2,1)S(1)}, bf16[384,512]{1,0:T(8,128)(2,1)S(1)}, u32[]{:S(2)}, u32[]{:S(2)}) collective-permute-start(bf16[384,512]{1,0:T(8,128)(2,1)S(1)} %get-tuple-element.34.refs_0_), channel_id=1, source_target_pairs={{0,2},{1,3},{2,0},{3,1},{4,6},{5,7},{6,4},{7,5},{8,10},{9,11},{10,... | collective-permute-start | bytes 1179656 | tf_op jit(solution)/shard_map/ppermute | solution.py:176
  28.1 14.6 %collective-permute-start.6 = (bf16[384,512]{1,0:T(8,128)(2,1)S(1)}, bf16[384,512]{1,0:T(8,128)(2,1)S(1)}, u32[]{:S(2)}, u32[]{:S(2)}) collective-permute-start(bf16[384,512]{1,0:T(8,128)(2,1)S(1)} %get-tuple-element.35.refs_1_), channel_id=1, source_target_pairs={{0,4},{1,5},{2,6},{3,7},{4,0},{5,1},{6,2},{7,3},{8,12},{9,13},{10,... | collective-permute-start | bytes 1179656 | tf_op jit(solution)/shard_map/ppermute | solution.py:176
  37.4 22.4 %collective-permute-start.4 = (bf16[768,512]{1,0:T(8,128)(2,1)S(1)}, bf16[768,512]{1,0:T(8,128)(2,1)S(1)}, u32[]{:S(2)}, u32[]{:S(2)}) collective-permute-start(bf16[768,512]{1,0:T(8,128)(2,1)S(1)} %shard_map.57), channel_id=1, source_target_pairs={{0,8},{24,16},{1,9},{25,17},{2,10},{26,18},{3,11},{27,19},{4,12},{... | collective-permute-start | bytes 2359304 | tf_op jit(solution)/shard_map/ppermute | solution.py:199
  43.6 11.0 %collective-permute-start.7 = (bf16[384,512]{1,0:T(8,128)(2,1)S(1)}, bf16[384,512]{1,0:T(8,128)(2,1)S(1)}, u32[]{:S(2)}, u32[]{:S(2)}) collective-permute-start(bf16[384,512]{1,0:T(8,128)(2,1)S(1)} %get-tuple-element.36), channel_id=1, source_target_pairs={{0,4},{1,5},{2,6},{3,7},{4,0},{5,1},{6,2},{7,3},{8,12},{9,13},{10,... | collective-permute-start | bytes 1179656 | tf_op jit(solution)/shard_map/ppermute | solution.py:176
  44.3 11.7 %collective-permute-start.8 = (bf16[384,512]{1,0:T(8,128)(2,1)S(1)}, bf16[384,512]{1,0:T(8,128)(2,1)S(1)}, u32[]{:S(2)}, u32[]{:S(2)}) collective-permute-start(bf16[384,512]{1,0:T(8,128)(2,1)S(1)} %get-tuple-element.37), channel_id=1, source_target_pairs={{0,2},{1,3},{2,0},{3,1},{4,6},{5,7},{6,4},{7,5},{8,10},{9,11},{10,... | collective-permute-start | bytes 1179656 | tf_op jit(solution)/shard_map/ppermute | solution.py:176
  47.5 29.1 %collective-permute-start.22 = (bf16[768,512]{1,0:T(8,128)(2,1)S(1)}, bf16[768,512]{1,0:T(8,128)(2,1)S(1)}, u32[]{:S(2)}, u32[]{:S(2)}) collective-permute-start(bf16[768,512]{1,0:T(8,128)(2,1)S(1)} %get-tuple-element.51), channel_id=1, source_target_pairs={{0,8},{8,16},{1,9},{9,17},{2,10},{10,18},{3,11},{11,19},{4,12},{12... | collective-permute-start | bytes 2359304 | tf_op jit(solution)/shard_map/ppermute | solution.py:199
  54.6 8.7 %collective-permute-start.11 = (bf16[384,512]{1,0:T(8,128)(2,1)S(1)}, bf16[384,512]{1,0:T(8,128)(2,1)S(1)}, u32[]{:S(2)}, u32[]{:S(2)}) collective-permute-start(bf16[384,512]{1,0:T(8,128)(2,1)S(1)} %get-tuple-element.40.refs_0_), channel_id=1, source_target_pairs={{0,2},{1,3},{2,0},{3,1},{4,6},{5,7},{6,4},{7,5},{8,10},{9,11},{10,... | collective-permute-start | bytes 1179656 | tf_op jit(solution)/shard_map/ppermute | solution.py:176
  54.7 24.0 %collective-permute-start.23 = (bf16[768,512]{1,0:T(8,128)(2,1)S(1)}, bf16[768,512]{1,0:T(8,128)(2,1)S(1)}, u32[]{:S(2)}, u32[]{:S(2)}) collective-permute-start(bf16[768,512]{1,0:T(8,128)(2,1)S(1)} %get-tuple-element.52), channel_id=1, source_target_pairs={{24,16},{16,8},{25,17},{17,9},{26,18},{18,10},{27,19},{19,11},{28,... | collective-permute-start | bytes 2359304 | tf_op jit(solution)/shard_map/ppermute | solution.py:199
  56.0 11.9 %collective-permute-start.12 = (bf16[384,512]{1,0:T(8,128)(2,1)S(1)}, bf16[384,512]{1,0:T(8,128)(2,1)S(1)}, u32[]{:S(2)}, u32[]{:S(2)}) collective-permute-start(bf16[384,512]{1,0:T(8,128)(2,1)S(1)} %get-tuple-element.41.refs_1_), channel_id=1, source_target_pairs={{0,4},{1,5},{2,6},{3,7},{4,0},{5,1},{6,2},{7,3},{8,12},{9,13},{10,... | collective-permute-start | bytes 1179656 | tf_op jit(solution)/shard_map/ppermute | solution.py:176
  62.0 29.3 %collective-permute-start.10 = (bf16[768,512]{1,0:T(8,128)(2,1)S(1)}, bf16[768,512]{1,0:T(8,128)(2,1)S(1)}, u32[]{:S(2)}, u32[]{:S(2)}) collective-permute-start(bf16[768,512]{1,0:T(8,128)(2,1)S(1)} %get-tuple-element.39), channel_id=1, source_target_pairs={{24,16},{16,8},{25,17},{17,9},{26,18},{18,10},{27,19},{19,11},{28,... | collective-permute-start | bytes 2359304 | tf_op jit(solution)/shard_map/ppermute | solution.py:199
  63.3 30.1 %collective-permute-start.9 = (bf16[768,512]{1,0:T(8,128)(2,1)S(1)}, bf16[768,512]{1,0:T(8,128)(2,1)S(1)}, u32[]{:S(2)}, u32[]{:S(2)}) collective-permute-start(bf16[768,512]{1,0:T(8,128)(2,1)S(1)} %get-tuple-element.38), channel_id=1, source_target_pairs={{0,8},{8,16},{1,9},{9,17},{2,10},{10,18},{3,11},{11,19},{4,12},{12... | collective-permute-start | bytes 2359304 | tf_op jit(solution)/shard_map/ppermute | solution.py:199
  68.8 15.8 %collective-permute-start.13 = (bf16[384,512]{1,0:T(8,128)(2,1)S(1)}, bf16[384,512]{1,0:T(8,128)(2,1)S(1)}, u32[]{:S(2)}, u32[]{:S(2)}) collective-permute-start(bf16[384,512]{1,0:T(8,128)(2,1)S(1)} %get-tuple-element.42), channel_id=1, source_target_pairs={{0,4},{1,5},{2,6},{3,7},{4,0},{5,1},{6,2},{7,3},{8,12},{9,13},{10,... | collective-permute-start | bytes 1179656 | tf_op jit(solution)/shard_map/ppermute | solution.py:176
  76.6 10.8 %collective-permute-start.14 = (bf16[384,512]{1,0:T(8,128)(2,1)S(1)}, bf16[384,512]{1,0:T(8,128)(2,1)S(1)}, u32[]{:S(2)}, u32[]{:S(2)}) collective-permute-start(bf16[384,512]{1,0:T(8,128)(2,1)S(1)} %get-tuple-element.43), channel_id=1, source_target_pairs={{0,2},{1,3},{2,0},{3,1},{4,6},{5,7},{6,4},{7,5},{8,10},{9,11},{10,... | collective-permute-start | bytes 1179656 | tf_op jit(solution)/shard_map/ppermute | solution.py:176
  82.5 27.8 %collective-permute-start.24 = (bf16[768,512]{1,0:T(8,128)(2,1)S(1)}, bf16[768,512]{1,0:T(8,128)(2,1)S(1)}, u32[]{:S(2)}, u32[]{:S(2)}) collective-permute-start(bf16[768,512]{1,0:T(8,128)(2,1)S(1)} %get-tuple-element.53), channel_id=1, source_target_pairs={{0,8},{8,16},{16,24},{1,9},{9,17},{17,25},{2,10},{10,18},{18,26},{... | collective-permute-start | bytes 2359304 | tf_op jit(solution)/shard_map/ppermute | solution.py:199
  84.6 17.7 %collective-permute-start.17 = (bf16[384,512]{1,0:T(8,128)(2,1)S(1)}, bf16[384,512]{1,0:T(8,128)(2,1)S(1)}, u32[]{:S(2)}, u32[]{:S(2)}) collective-permute-start(bf16[384,512]{1,0:T(8,128)(2,1)S(1)} %get-tuple-element.46.refs_0_), channel_id=1, source_target_pairs={{0,2},{1,3},{2,0},{3,1},{4,6},{5,7},{6,4},{7,5},{8,10},{9,11},{10,... | collective-permute-start | bytes 1179656 | tf_op jit(solution)/shard_map/ppermute | solution.py:176
  87.4 16.8 %collective-permute-start.18 = (bf16[384,512]{1,0:T(8,128)(2,1)S(1)}, bf16[384,512]{1,0:T(8,128)(2,1)S(1)}, u32[]{:S(2)}, u32[]{:S(2)}) collective-permute-start(bf16[384,512]{1,0:T(8,128)(2,1)S(1)} %get-tuple-element.47.refs_1_), channel_id=1, source_target_pairs={{0,4},{1,5},{2,6},{3,7},{4,0},{5,1},{6,2},{7,3},{8,12},{9,13},{10,... | collective-permute-start | bytes 1179656 | tf_op jit(solution)/shard_map/ppermute | solution.py:176
  91.3 25.5 %collective-permute-start.25 = (bf16[768,512]{1,0:T(8,128)(2,1)}, bf16[768,512]{1,0:T(8,128)(2,1)}, u32[]{:S(2)}, u32[]{:S(2)}) collective-permute-start(bf16[768,512]{1,0:T(8,128)(2,1)} %get-tuple-element.54), channel_id=1, source_target_pairs={{24,16},{16,8},{8,0},{25,17},{17,9},{9,1},{26,18},{18,10},{10,2},{... | collective-permute-start | bytes 2359304 | tf_op jit(solution)/shard_map/ppermute | solution.py:199
  97.0 13.8 %copy-start.6 = (s32[8]{0:T(128)S(1)}, s32[8]{0:T(128)}, u32[]{:S(2)}) copy-start(s32[8]{0:T(128)} %refs_2_.21) | copy-start | bytes 100
  97.0 19.8 %copy-start.8 = (s32[1,8]{1,0:T(1,128)S(1)}, s32[1,8]{1,0:T(1,128)}, u32[]{:S(2)}) copy-start(s32[1,8]{1,0:T(1,128)} %refs_0_.21) | copy-start | bytes 100
  97.0 26.1 %collective-permute-start.15 = (bf16[768,512]{1,0:T(8,128)(2,1)}, bf16[768,512]{1,0:T(8,128)(2,1)}, u32[]{:S(2)}, u32[]{:S(2)}) collective-permute-start(bf16[768,512]{1,0:T(8,128)(2,1)} %get-tuple-element.44), channel_id=1, source_target_pairs={{0,8},{8,16},{16,24},{1,9},{9,17},{17,25},{2,10},{10,18},{18,26},{... | collective-permute-start | bytes 2359304 | tf_op jit(solution)/shard_map/ppermute | solution.py:199
  102.3 25.1 %collective-permute-start.16 = (bf16[768,512]{1,0:T(8,128)(2,1)}, bf16[768,512]{1,0:T(8,128)(2,1)}, u32[]{:S(2)}, u32[]{:S(2)}) collective-permute-start(bf16[768,512]{1,0:T(8,128)(2,1)} %get-tuple-element.45), channel_id=1, source_target_pairs={{24,16},{16,8},{8,0},{25,17},{17,9},{9,1},{26,18},{18,10},{10,2},{... | collective-permute-start | bytes 2359304 | tf_op jit(solution)/shard_map/ppermute | solution.py:199
  105.9 15.7 %collective-permute-start.19 = (bf16[384,512]{1,0:T(8,128)(2,1)}, bf16[384,512]{1,0:T(8,128)(2,1)S(1)}, u32[]{:S(2)}, u32[]{:S(2)}) collective-permute-start(bf16[384,512]{1,0:T(8,128)(2,1)} %get-tuple-element.48), channel_id=1, source_target_pairs={{0,4},{1,5},{2,6},{3,7},{4,0},{5,1},{6,2},{7,3},{8,12},{9,13},{10,... | collective-permute-start | bytes 1179656 | tf_op jit(solution)/shard_map/ppermute | solution.py:176
  110.3 11.3 %collective-permute-start.20 = (bf16[384,512]{1,0:T(8,128)(2,1)}, bf16[384,512]{1,0:T(8,128)(2,1)}, u32[]{:S(2)}, u32[]{:S(2)}) collective-permute-start(bf16[384,512]{1,0:T(8,128)(2,1)} %get-tuple-element.49), channel_id=1, source_target_pairs={{0,2},{1,3},{2,0},{3,1},{4,6},{5,7},{6,4},{7,5},{8,10},{9,11},{10,... | collective-permute-start | bytes 1179656 | tf_op jit(solution)/shard_map/ppermute | solution.py:176
  116.9 2.2 %copy-start.2 = (bf16[1024,2048]{1,0:T(8,128)(2,1)S(1)}, bf16[1024,2048]{1,0:T(8,128)(2,1)}, u32[]{:S(2)}) copy-start(bf16[1024,2048]{1,0:T(8,128)(2,1)} %refs_4_.21) | copy-start | bytes 12582916

commit v2 on v0

v2 whole, which is shorter than its diff:
```python
import functools

import jax
import jax.numpy as jnp
from jax import lax
from jax.experimental import pallas as pl
from jax.experimental.pallas import tpu as pltpu
from jax.sharding import PartitionSpec as P

EXP_DEV = 2
COLD, HOT, REPLICA = 0, 1, 2
SMEM = pl.BlockSpec(memory_space=pltpu.SMEM)
VMEM = pl.BlockSpec(memory_space=pltpu.VMEM)
ANY = pl.BlockSpec(memory_space=pl.ANY)
HBM = pl.BlockSpec(memory_space=pltpu.HBM)


def params(mib):
    return pltpu.CompilerParams(vmem_limit_bytes=mib << 20)


def flip_of(k, quarter, phase):
    return 1 + (k % quarter + phase) % 2


def partner(k, quarter, flip):
    return jnp.bitwise_xor(k // quarter, flip) * quarter + k % quarter


F_HOT, F_GOES, F_PASSES, F_ARRIVES, F_COUNT = 0, 1, 2, 3, 4


def write_flags(flags, slots, counts, placement, blocks, holders):
    here = lax.axis_index("expert")
    quarter = holders // 4
    group, place = lax.rem(here, quarter), lax.div(here, quarter)

    def at(flip):
        return jnp.bitwise_xor(place, flip) * quarter + group

    def home(owner):
        return lax.div(owner, EXP_DEV)

    odd = lax.rem(group, 2)
    first, second = 1 + odd, 2 - odd
    mine, sender = placement[here], placement[at(first)]
    hot = jnp.int32(EXP_DEV - 1)
    for flip in (3, 1, 2):
        owner = placement[at(flip)]
        hot = jnp.where(home(owner) == here, lax.rem(owner, EXP_DEV), hot)
    flags[blocks + F_HOT] = hot
    flags[blocks + F_GOES] = (home(mine) == at(second)).astype(jnp.int32)
    flags[blocks + F_PASSES] = (home(sender) == at(second)).astype(jnp.int32)
    flags[blocks + F_ARRIVES] = (home(sender) == here).astype(jnp.int32)
    for b in range(blocks):
        slot = slots[0, b]
        local = jnp.where((slot == EXP_DEV) & (home(mine) == here), lax.rem(mine, EXP_DEV), slot)
        kind = jnp.where(local == EXP_DEV, REPLICA, jnp.where(local == hot, HOT, COLD))
        flags[b] = jnp.where(b < counts[0], kind, -1)


def products(jobs, blocks, flags, hidden_v, grad_v, total, outs, wait):
    rows = hidden_v.shape[0] // blocks
    for j, (kind, _) in enumerate(jobs):
        wait(j)
        total[...] = jnp.zeros_like(total)

        @pl.loop(0, blocks)
        def _(b):
            @pl.when(flags[b] == kind)
            def _():
                at = pl.ds(pl.multiple_of(b * rows, rows), rows)
                total[...] += lax.dot_general(
                    hidden_v[at, :], grad_v[j, at, :], (((0,), (0,)), ((), ())), preferred_element_type=jnp.float32
                )

        outs[j][...] = total[...].astype(outs[j].dtype)


def fetches(jobs, hidden, grad, hidden_v, grad_v, sem):
    width = grad_v.shape[2]
    copies = [pltpu.make_async_copy(hidden, hidden_v, sem.at[0])]
    for j, (_, mask) in enumerate(jobs):
        begin = pl.multiple_of(jnp.bitwise_xor(lax.axis_index("dp"), mask) * width, width)
        copies.append(pltpu.make_async_copy(grad.at[:, pl.ds(begin, width)], grad_v.at[j], sem.at[1 + j]))
    for copy in copies:
        copy.start()

    def wait(j):
        if j == 0:
            copies[0].wait()
        copies[1 + j].wait()

    return wait


def opening_kernel(jobs, blocks, holders, slots, counts, placement, hidden, grad, flags, *refs):
    outs = refs[: len(jobs)]
    slots_s, counts_s, placement_s, hidden_v, grad_v, total, sem, small = refs[len(jobs) :]
    scalars = [
        pltpu.make_async_copy(source, target, small.at[i])
        for i, (source, target) in enumerate(((slots, slots_s), (counts, counts_s), (placement, placement_s)))
    ]
    for copy in scalars:
        copy.start()
    wait = fetches(jobs, hidden, grad, hidden_v, grad_v, sem)
    for copy in scalars:
        copy.wait()
    write_flags(flags, slots_s, counts_s, placement_s, blocks, holders)
    products(jobs, blocks, flags, hidden_v, grad_v, total, outs, wait)


def product_kernel(jobs, blocks, flags, hidden, grad, *refs):
    outs = refs[1 : 1 + len(jobs)]
    hidden_v, grad_v, total, sem = refs[1 + len(jobs) :]
    wait = fetches(jobs, hidden, grad, hidden_v, grad_v, sem)
    products(jobs, blocks, flags, hidden_v, grad_v, total, outs, wait)


def product_scratch(jobs, hidden, width):
    return [
        pltpu.VMEM(hidden.shape, hidden.dtype),
        pltpu.VMEM((len(jobs), hidden.shape[0], width), hidden.dtype),
        pltpu.VMEM((hidden.shape[1], width), jnp.float32),
        pltpu.SemaphoreType.DMA((1 + len(jobs),)),
    ]


def product_cost(jobs, hidden, width):
    rows, ff = hidden.shape
    return pl.CostEstimate(
        flops=2 * len(jobs) * rows * ff * width,
        bytes_accessed=2 * (hidden.size + len(jobs) * (rows + ff) * width),
        transcendentals=0,
    )


def combine_kernel(recipe, blocks, n_in, flags, *refs):
    arrays, outs = refs[:n_in], refs[n_in + 1 :]
    for out, terms in zip(outs, recipe):
        total = None
        for position, flag in terms:
            value = arrays[position][...].astype(jnp.float32)
            if flag is not None:
                value = jnp.where(flags[blocks + flag] == 1, value, jnp.zeros_like(value))
            total = value if total is None else total + value
        out[...] = total.astype(out.dtype)


def place_kernel(blocks, is_hot, n_in, flags, *refs):
    arrays, out = refs[:n_in], refs[n_in + 1]
    buffer, sem = refs[n_in + 2 :]
    chunks = buffer.shape[0]
    rows = buffer.shape[1]
    hot = flags[blocks + F_HOT]
    slot = hot if is_hot else EXP_DEV - 1 - hot
    copies = []
    for c in range(chunks):
        at = slice(c * rows, (c + 1) * rows)
        total = arrays[0][at, :].astype(jnp.float32)
        for array in arrays[1:]:
            total = total + array[at, :].astype(jnp.float32)
        buffer[c] = total.astype(buffer.dtype)
        copies.append(pltpu.make_async_copy(buffer.at[c], out.at[slot, pl.ds(c * rows, rows), :], sem.at[c]))
        copies[-1].start()
    for copy in copies:
        copy.wait()


def body(hidden, grad, slots, counts, placement):
    n, holders = lax.axis_size("dp"), lax.axis_size("expert")
    (rows, ff), width, blocks = hidden.shape, grad.shape[1] // n, slots.shape[1]
    piece = jax.ShapeDtypeStruct((ff, width), jnp.bfloat16)
    quarter = holders // 4
    chain = []

    def opening(jobs):
        flags, *outs = pl.pallas_call(
            functools.partial(opening_kernel, jobs, blocks, holders),
            out_shape=[jax.ShapeDtypeStruct((blocks + F_COUNT,), jnp.int32)] + [piece] * len(jobs),
            in_specs=[HBM] * 5,
            out_specs=[SMEM] + [VMEM] * len(jobs),
            scratch_shapes=[pltpu.SMEM(a.shape, a.dtype) for a in (slots, counts, placement)]
            + product_scratch(jobs, hidden, width)
            + [pltpu.SemaphoreType.DMA((3,))],
            compiler_params=params(32),
            cost_estimate=product_cost(jobs, hidden, width),
        )(slots, counts, placement, hidden, grad)
        chain.append(outs[0])
        return flags, outs

    def product(flags, *jobs):
        outs = pl.pallas_call(
            functools.partial(product_kernel, jobs, blocks),
            out_shape=[piece] * len(jobs),
            in_specs=[SMEM, HBM, HBM, ANY],
            out_specs=[VMEM] * len(jobs),
            scratch_shapes=product_scratch(jobs, hidden, width),
            compiler_params=params(32),
            cost_estimate=product_cost(jobs, hidden, width),
        )(flags, hidden, grad, chain[-1])
        chain.append(outs[0])
        return outs

    def combine(flags, arrays, recipe):
        outs = pl.pallas_call(
            functools.partial(combine_kernel, recipe, blocks, len(arrays)),
            out_shape=[piece] * len(recipe),
            in_specs=[SMEM] + [VMEM] * len(arrays) + [ANY],
            out_specs=[VMEM] * len(recipe),
            compiler_params=params(32),
            cost_estimate=pl.CostEstimate(
                flops=len(arrays) * ff * width, bytes_accessed=2 * (len(arrays) + len(recipe)) * ff * width, transcendentals=0
            ),
        )(flags, *arrays, chain[-1])
        chain.append(outs[0])
        return outs

    def place(flags, arrays, before, is_hot):
        chunks = 4
        out = pl.pallas_call(
            functools.partial(place_kernel, blocks, is_hot, len(arrays)),
            out_shape=jax.ShapeDtypeStruct((EXP_DEV, ff, width), jnp.bfloat16),
            in_specs=[SMEM] + [VMEM] * len(arrays) + [ANY],
            out_specs=HBM,
            scratch_shapes=[pltpu.VMEM((chunks, ff // chunks, width), jnp.bfloat16), pltpu.SemaphoreType.DMA((chunks,))],
            input_output_aliases={1 + len(arrays): 0} if is_hot else {},
            compiler_params=params(32),
            cost_estimate=pl.CostEstimate(flops=3 * ff * width, bytes_accessed=8 * ff * width, transcendentals=0),
        )(flags, *arrays, before)
        chain.append(out)
        return out

    def plane(x, phase):
        pairs = []
        for k in range(holders):
            place_of, group = k // quarter, k % quarter
            pairs.append((k, (place_of ^ (1 + (group + phase) % 2)) * quarter + group))
        return lax.ppermute(x, "expert", pairs)

    def outer(x):
        return lax.ppermute(x, "dp", [(0, 1), (n - 1, n - 2)])

    def middle(x):
        return lax.ppermute(x, "dp", [(1, 2), (2, 1)])

    def both(x):
        return lax.ppermute(x, "dp", [(0, 1), (1, 0), (2, 3), (3, 2)])

    relay_of = lambda own, came: [(own, F_GOES), (came, F_PASSES)]
    add_of = lambda own, came, relayed: [(own, None), (came, F_ARRIVES), (relayed, None)]

    flags, (c3,) = opening([(COLD, 3)])
    o_c1 = outer(c3)
    (r3,) = product(flags, (REPLICA, 3))
    a1 = plane(r3, 0)
    c2, h3 = product(flags, (COLD, 2), (HOT, 3))
    o_c2 = outer(c2)
    (s3,) = combine(flags, [r3, a1], [relay_of(0, 1)])
    a2 = plane(s3, 1)
    r2, h2 = product(flags, (REPLICA, 2), (HOT, 2))
    (y,) = combine(flags, [c2, o_c1], [[(0, None), (1, None)]])
    m_c1 = middle(y)
    (h3,) = combine(flags, [h3, a1, a2], [add_of(0, 1, 2)])
    o_h1 = outer(h3)
    b1 = plane(r2, 0)
    r1, r0 = product(flags, (REPLICA, 1), (REPLICA, 0))
    (s2,) = combine(flags, [r2, b1], [relay_of(0, 1)])
    b2 = plane(s2, 1)
    c1, c0 = product(flags, (COLD, 1), (COLD, 0))
    (y,) = combine(flags, [c3, o_c2], [[(0, None), (1, None)]])
    m_c2 = middle(y)
    h1, h0 = product(flags, (HOT, 1), (HOT, 0))
    (h2,) = combine(flags, [h2, b1, b2], [add_of(0, 1, 2)])
    o_h2 = outer(h2)
    d1 = plane(jnp.stack([r1, r0]), 0)
    (x_c3,) = combine(flags, [c1, m_c1], [[(0, None), (1, None)]])
    (y,) = combine(flags, [h2, o_h1], [[(0, None), (1, None)]])
    m_h1 = middle(y)
    x_c3 = both(x_c3)
    s1, s0 = combine(flags, [r1, r0, d1[0], d1[1]], [relay_of(0, 2), relay_of(1, 3)])
    d2 = plane(jnp.stack([s1, s0]), 1)
    (y,) = combine(flags, [h3, o_h2], [[(0, None), (1, None)]])
    m_h2 = middle(y)
    x_h3, h0 = combine(
        flags, [h1, h0, d1[0], d1[1], d2[0], d2[1], m_h1], [add_of(0, 2, 4) + [(6, None)], add_of(1, 3, 5)]
    )
    x_h3 = both(x_h3)
    out = place(flags, [c0, m_c2, x_c3], chain[-1], False)
    return place(flags, [h0, m_h2, x_h3], out, True)


def solution(mesh):
    in_specs = (
        P(("dp", "expert"), None),
        P(("dp", "expert"), None),
        P(("dp", "expert"), None),
        P(("dp", "expert")),
        P(),
    )
    out_specs = P("expert", None, "dp")
    return jax.shard_map(body, mesh=mesh, in_specs=in_specs, out_specs=out_specs, check_vma=False)
```

time: 288 us -> 140 us (0.49)
  blocking collectives: 195 us -> 0 us
  waiting for transfers between devices: 21.3 us -> 70.5 us
  Pallas kernels: 0 us -> 27.2 us
  starting transfers between devices: 9.96 us -> 33.7 us
  between operations: 22.3 us -> 0.97 us
  matrix products: 14.8 us -> 0 us
  local copies, waits for them, and re-layouts: 15.8 us -> 5.83 us
  other arithmetic: 5.54 us -> 0.29 us
    unnamed x1 -> x0, blocking collectives: 183 us -> none
    ppermute x3 -> x16, waiting for transfers between devices: 20.6 us -> 70.5 us  [the longest x4 32.5 us: outer(): return lax.ppermute(x, 'dp', [(0, 1), (n - 1, n - 2)])]
    ppermute x3 -> x16, starting transfers between devices: 4.5 us -> 33.7 us  [the longest x4 16.8 us: middle(): return lax.ppermute(x, 'dp', [(1, 2), (2, 1)])]
    pallas_call x0 -> x20, Pallas kernels: none -> 27.2 us  [the longest x6 13.3 us: product(): pl.pallas_call(functools.partial(product_kernel, jobs, blocks), out_shape...]
    dot_general x3 -> x0, matrix products: 14.8 us -> none  [slot_products(): lax.dot_general(masked, grad_out, (((0,), (0,)), ((), ())), preferred_ele...]
    all_gather x1 -> x0, blocking collectives: 11.1 us -> none  [body(): lax.all_gather(block_slot, 'dp', axis=0, tiled=True)]
    all_to_all x1 -> x0, local copies, waits for them, and re-layouts: 6.26 us -> none  [body(): lax.all_to_all(grad_out, 'dp', split_axis=1, concat_axis=0, tiled=True)]
    convert_element_type x6 -> x0, other arithmetic: 5.5 us -> none  [the longest x2 2.61 us: slot_products(): row_mask = jnp.repeat(chosen, rows_per).astype(hidden.dtype)]
  transfers between devices with their start and end apart: 5 -> 16, of which waited for: 2 -> 8; matrix products, arithmetic and copies ran while one was open for 9% -> 0% of each run, Pallas kernels for 0% -> 15%
where the time goes in v2:
time: 140 us; the launch traced here: 139 us
  waiting for transfers between devices  70.5 us (50%)
  starting transfers between devices  33.7 us (24%)
  Pallas kernels  27.2 us (19%)
  local copies, waits for them, and re-layouts  5.83 us (4%)
    ppermute x4, waiting for transfers between devices, outer(): return lax.ppermute(x, 'dp', [(0, 1), (n - 1, n - 2)])  32.5 us
    ppermute x4, waiting for transfers between devices, middle(): return lax.ppermute(x, 'dp', [(1, 2), (2, 1)])  21.9 us
    ppermute x4, starting transfers between devices, middle(): return lax.ppermute(x, 'dp', [(1, 2), (2, 1)])  16.8 us
    ppermute x6, waiting for transfers between devices, plane(): return lax.ppermute(x, 'expert', pairs)  16.1 us
    pallas_call x6, Pallas kernels, product(): pl.pallas_call(functools.partial(product_kernel, jobs, blocks), out_shape...  13.3 us
    ppermute x6, starting transfers between devices, plane(): return lax.ppermute(x, 'expert', pairs)  11.6 us
    pallas_call x11, Pallas kernels, combine(): pl.pallas_call(functools.partial(combine_kernel, recipe, blocks, len(arra...  9.41 us
    unnamed x12, local copies, waits for them, and re-layouts  5.62 us
  transfers between devices with their start and end apart: 16, of which 8 were waited for; matrix products, arithmetic and copies ran while one was open for 0% of the time, Pallas kernels for 15%

profile of v2, /device:TPU:8, one launch (start us, length us, event | category | flops | bytes accessed | tf_op | source)
XLA Modules:
  0.0 138.5 jit_solution(18188085510247646549)
XLA Ops:
  0.7 2.2 %copy-done = bf16[1024,2048]{1,0:T(8,128)(2,1)S(1)} copy-done((bf16[1024,2048]{1,0:T(8,128)(2,1)S(1)}, bf16[1024,2048]{1,0:T(8,128)(2,1)}, u32[]{:S(2)}) %copy-start) | copy-done | bytes 4194328
  2.8 1.4 %copy-done.2 = bf16[1024,768]{1,0:T(8,128)(2,1)S(1)} copy-done((bf16[1024,768]{1,0:T(8,128)(2,1)S(1)}, bf16[1024,768]{1,0:T(8,128)(2,1)}, u32[]{:S(2)}) %copy-start.2) | copy-done | bytes 1572888
  4.3 0.7 copy-done.4
  4.9 0.7 copy-done.5
  5.6 1.5 %shard_map.55 = (s32[12]{0:T(128)S(1)}, bf16[768,512]{1,0:T(8,128)(2,1)S(1)}) custom-call(s32[1,8]{1,0:T(1,128)S(1)} %copy-done.4, s32[1]{0:T(128)S(6)} %copy.8.counts, s32[8]{0:T(128)S(1)} %copy-done.5, bf16[1024,768]{1,0:T(8,128)(2,1)S(1)} %copy-done.2, bf16[1024,2048]{1,0:T(8,128)(2,1)S(1)} %copy-done), custom_call_target="tpu_custom_call" | custom-call | flops 805306368 | bytes 3407872 | tf_op jit(solution)/shard_map/pallas_call | solution.py:178
  7.0 0.7 copy-done.1
  7.7 1.8 %shard_map.56.refs_0_ = bf16[768,512]{1,0:T(8,128)(2,1)S(1)} custom-call(s32[12]{0:T(128)S(1)} %get-tuple-element.21.flags, bf16[1024,768]{1,0:T(8,128)(2,1)S(1)} %copy-done.2, bf16[1024,2048]{1,0:T(8,128)(2,1)S(1)} %copy-done.1, bf16[768,512]{1,0:T(8,128)(2,1)S(1)} %get-tuple-element.22.refs_0_), custom_call_target="tpu_custom_call" | custom-call | flops 805306368 | bytes 3407872 | tf_op jit(solution)/shard_map/pallas_call | solution.py:193
  9.6 1.2 collective-permute-start.1
  10.8 1.3 collective-permute-start.4
  12.1 1.9 %shard_map.57 = (bf16[768,512]{1,0:T(8,128)(2,1)S(1)}, bf16[768,512]{1,0:T(8,128)(2,1)S(1)}) custom-call(s32[12]{0:T(128)S(1)} %get-tuple-element.21.flags, bf16[1024,768]{1,0:T(8,128)(2,1)S(1)} %copy-done.2, bf16[1024,2048]{1,0:T(8,128)(2,1)S(1)} %copy-done.1, bf16[768,512]{1,0:T(8,128)(2,1)S(1)} %shard_map.56.refs_0_), custom_call_target="tpu_custom_call" | custom-call | flops 1610612736 | bytes 5242880 | tf_op jit(solution)/shard_map/pallas_call | solution.py:193
  14.1 7.6 %collective-permute-done.1.refs_1_ = bf16[768,512]{1,0:T(8,128)(2,1)S(1)} collective-permute-done((bf16[768,512]{1,0:T(8,128)(2,1)S(1)}, bf16[768,512]{1,0:T(8,128)(2,1)S(1)}, u32[]{:S(2)}, u32[]{:S(2)}) %collective-permute-start.1) | collective-permute-done | bytes 786464 | tf_op jit(solution)/shard_map/ppermute | solution.py:239
  21.7 0.8 shard_map.58.refs_0_
  22.5 1.6 %collective-permute-start.3 = (bf16[768,512]{1,0:T(8,128)(2,1)S(1)}, bf16[768,512]{1,0:T(8,128)(2,1)S(1)}, u32[]{:S(2)}, u32[]{:S(2)}) collective-permute-start(bf16[768,512]{1,0:T(8,128)(2,1)S(1)} %shard_map.58.refs_0_), channel_id=1, source_target_pairs={{0,4},{1,3},{2,6},{3,1},{4,0},{5,7},{6,2},{7,5},{8,12},{9,11},{10,... | collective-permute-start | bytes 2359304 | tf_op jit(solution)/shard_map/ppermute | solution.py:239
  24.1 2.7 %shard_map.59 = (bf16[768,512]{1,0:T(8,128)(2,1)S(1)}, bf16[768,512]{1,0:T(8,128)(2,1)S(1)}) custom-call(s32[12]{0:T(128)S(1)} %get-tuple-element.21.flags, bf16[1024,768]{1,0:T(8,128)(2,1)S(1)} %copy-done.3, bf16[1024,2048]{1,0:T(8,128)(2,1)S(1)} %copy-done.1, bf16[768,512]{1,0:T(8,128)(2,1)S(1)} %shard_map.58.refs_0_), custom_call_target="tpu_custom_call" | custom-call | flops 1610612736 | bytes 5242880 | tf_op jit(solution)/shard_map/pallas_call | solution.py:193
  26.8 1.2 collective-permute-start.2
  27.9 4.1 %collective-permute-done.4.refs_1_ = bf16[768,512]{1,0:T(8,128)(2,1)S(1)} collective-permute-done((bf16[768,512]{1,0:T(8,128)(2,1)S(1)}, bf16[768,512]{1,0:T(8,128)(2,1)S(1)}, u32[]{:S(2)}, u32[]{:S(2)}) %collective-permute-start.4) | collective-permute-done | bytes 786464 | tf_op jit(solution)/shard_map/ppermute | solution.py:242
  32.1 0.7 shard_map.60.refs_3_
  32.8 8.5 %collective-permute-done.3.refs_2_ = bf16[768,512]{1,0:T(8,128)(2,1)S(1)} collective-permute-done((bf16[768,512]{1,0:T(8,128)(2,1)S(1)}, bf16[768,512]{1,0:T(8,128)(2,1)S(1)}, u32[]{:S(2)}, u32[]{:S(2)}) %collective-permute-start.3) | collective-permute-done | bytes 786464 | tf_op jit(solution)/shard_map/ppermute | solution.py:239
  41.3 0.9 shard_map.61.refs_0_
  42.2 3.0 %shard_map.62 = (bf16[768,512]{1,0:T(8,128)(2,1)S(1)}, bf16[768,512]{1,0:T(8,128)(2,1)S(1)}) custom-call(s32[12]{0:T(128)S(1)} %get-tuple-element.21.flags, bf16[1024,768]{1,0:T(8,128)(2,1)S(1)} %copy-done.3, bf16[1024,2048]{1,0:T(8,128)(2,1)S(1)} %copy-done.1, bf16[768,512]{1,0:T(8,128)(2,1)S(1)} %shard_map.61.refs_0_), custom_call_target="tpu_custom_call" | custom-call | flops 1610612736 | bytes 5242880 | tf_op jit(solution)/shard_map/pallas_call | solution.py:193
  45.4 1.9 %collective-permute-start.5 = (bf16[2,768,512]{2,1,0:T(8,128)(2,1)S(1)}, bf16[2,768,512]{2,1,0:T(8,128)(2,1)S(1)}, u32[]{:S(2)}, u32[]{:S(2)}) collective-permute-start(bf16[2,768,512]{2,1,0:T(8,128)(2,1)S(1)} %pad_maximum_fusion), channel_id=1, source_target_pairs={{0,2},{1,5},{2,0},{3,7},{4,6},{5,1},{6,4},{7,3},{8,10},{9,13},{10,... | collective-permute-start | bytes 4718600 | tf_op jit(solution)/shard_map/ppermute | solution.py:239
  47.3 1.3 collective-permute-start
  48.6 0.8 shard_map.63.refs_0_
  49.4 4.1 %collective-permute-start.6 = (bf16[768,512]{1,0:T(8,128)(2,1)S(1)}, bf16[768,512]{1,0:T(8,128)(2,1)S(1)}, u32[]{:S(2)}, u32[]{:S(2)}) collective-permute-start(bf16[768,512]{1,0:T(8,128)(2,1)S(1)} %shard_map.63.refs_0_), channel_id=1, source_target_pairs={{0,4},{1,3},{2,6},{3,1},{4,0},{5,7},{6,2},{7,5},{8,12},{9,11},{10,... | collective-permute-start | bytes 2359304 | tf_op jit(solution)/shard_map/ppermute | solution.py:239
  53.5 1.9 %collective-permute-start.8 = (bf16[768,512]{1,0:T(8,128)(2,1)S(1)}, bf16[768,512]{1,0:T(8,128)(2,1)S(1)}, u32[]{:S(2)}, u32[]{:S(2)}) collective-permute-start(bf16[768,512]{1,0:T(8,128)(2,1)S(1)} %shard_map.60.refs_3_), channel_id=1, source_target_pairs={{8,16},{16,8},{9,17},{17,9},{10,18},{18,10},{11,19},{19,11},{12,20... | collective-permute-start | bytes 2359304 | tf_op jit(solution)/shard_map/ppermute | solution.py:245
  55.4 1.3 collective-permute-start.7
  56.7 1.5 %shard_map.64 = (bf16[768,512]{1,0:T(8,128)(2,1)S(1)}, bf16[768,512]{1,0:T(8,128)(2,1)S(1)}) custom-call(s32[12]{0:T(128)S(1)} %get-tuple-element.21.flags, bf16[1024,768]{1,0:T(8,128)(2,1)S(1)} %copy-done.3, bf16[1024,2048]{1,0:T(8,128)(2,1)S(1)} %copy-done.1, bf16[768,512]{1,0:T(8,128)(2,1)S(1)} %shard_map.63.refs_0_), custom_call_target="tpu_custom_call" | custom-call | flops 1610612736 | bytes 5242880 | tf_op jit(solution)/shard_map/pallas_call | solution.py:193
  58.2 10.6 %collective-permute-done.refs_1_ = bf16[768,512]{1,0:T(8,128)(2,1)S(1)} collective-permute-done((bf16[768,512]{1,0:T(8,128)(2,1)S(1)}, bf16[768,512]{1,0:T(8,128)(2,1)S(1)}, u32[]{:S(2)}, u32[]{:S(2)}) %collective-permute-start) | collective-permute-done | bytes 786464 | tf_op jit(solution)/shard_map/ppermute | solution.py:242
  68.8 0.7 shard_map.65.refs_0_
  69.6 2.3 %shard_map.66 = (bf16[768,512]{1,0:T(8,128)(2,1)S(1)}, bf16[768,512]{1,0:T(8,128)(2,1)S(1)}) custom-call(s32[12]{0:T(128)S(1)} %get-tuple-element.21.flags, bf16[1024,768]{1,0:T(8,128)(2,1)S(1)} %copy-done.3, bf16[1024,2048]{1,0:T(8,128)(2,1)S(1)} %copy-done.1, bf16[768,512]{1,0:T(8,128)(2,1)S(1)} %shard_map.65.refs_0_), custom_call_target="tpu_custom_call" | custom-call | flops 1610612736 | bytes 5242880 | tf_op jit(solution)/shard_map/pallas_call | solution.py:193
  71.9 0.9 shard_map.67.refs_2_.refs_0_
  72.8 0.7 shard_map.68.refs_2_
  73.5 5.1 %collective-permute-done.7.refs_1_ = bf16[768,512]{1,0:T(8,128)(2,1)S(1)} collective-permute-done((bf16[768,512]{1,0:T(8,128)(2,1)S(1)}, bf16[768,512]{1,0:T(8,128)(2,1)S(1)}, u32[]{:S(2)}, u32[]{:S(2)}) %collective-permute-start.7) | collective-permute-done | bytes 786464 | tf_op jit(solution)/shard_map/ppermute | solution.py:242
  78.6 0.7 shard_map.69.refs_4_
  79.5 1.1 shard_map.70
  80.6 0.1 pad_maximum_fusion.1
  80.8 1.7 %collective-permute-start.9 = (bf16[2,768,512]{2,1,0:T(8,128)(2,1)S(1)}, bf16[2,768,512]{2,1,0:T(8,128)(2,1)S(1)}, u32[]{:S(2)}, u32[]{:S(2)}) collective-permute-start(bf16[2,768,512]{2,1,0:T(8,128)(2,1)S(1)} %pad_maximum_fusion.1), channel_id=1, source_target_pairs={{0,4},{1,3},{2,6},{3,1},{4,0},{5,7},{6,2},{7,5},{8,12},{9,11},{10,... | collective-permute-start | bytes 4718600 | tf_op jit(solution)/shard_map/ppermute | solution.py:239
  82.4 1.3 collective-permute-start.11
  83.7 6.5 %collective-permute-start.10 = (bf16[768,512]{1,0:T(8,128)(2,1)S(1)}, bf16[768,512]{1,0:T(8,128)(2,1)S(1)}, u32[]{:S(2)}, u32[]{:S(2)}) collective-permute-start(bf16[768,512]{1,0:T(8,128)(2,1)S(1)} %shard_map.69.refs_4_), channel_id=1, source_target_pairs={{8,16},{16,8},{9,17},{17,9},{10,18},{18,10},{11,19},{19,11},{12,20... | collective-permute-start | bytes 2359304 | tf_op jit(solution)/shard_map/ppermute | solution.py:245
  90.2 1.9 %collective-permute-start.14 = (bf16[768,512]{1,0:T(8,128)(2,1)S(1)}, bf16[768,512]{1,0:T(8,128)(2,1)S(1)}, u32[]{:S(2)}, u32[]{:S(2)}) collective-permute-start(bf16[768,512]{1,0:T(8,128)(2,1)S(1)} %shard_map.65.refs_0_), channel_id=1, source_target_pairs={{8,16},{16,8},{9,17},{17,9},{10,18},{18,10},{11,19},{19,11},{12,20... | collective-permute-start | bytes 2359304 | tf_op jit(solution)/shard_map/ppermute | solution.py:245
  92.2 12.6 %collective-permute-done.11.refs_1_ = bf16[768,512]{1,0:T(8,128)(2,1)S(1)} collective-permute-done((bf16[768,512]{1,0:T(8,128)(2,1)S(1)}, bf16[768,512]{1,0:T(8,128)(2,1)S(1)}, u32[]{:S(2)}, u32[]{:S(2)}) %collective-permute-start.11) | collective-permute-done | bytes 786464 | tf_op jit(solution)/shard_map/ppermute | solution.py:242
  104.8 0.7 shard_map.71.refs_7_
  105.5 6.5 %collective-permute-start.12 = (bf16[768,512]{1,0:T(8,128)(2,1)S(1)}, bf16[768,512]{1,0:T(8,128)(2,1)S(1)}, u32[]{:S(2)}, u32[]{:S(2)}) collective-permute-start(bf16[768,512]{1,0:T(8,128)(2,1)S(1)} %shard_map.71.refs_7_), channel_id=1, source_target_pairs={{8,16},{16,8},{9,17},{17,9},{10,18},{18,10},{11,19},{19,11},{12,20... | collective-permute-start | bytes 2359304 | tf_op jit(solution)/shard_map/ppermute | solution.py:245
  112.1 1.3 shard_map.72
  113.5 12.0 %collective-permute-done.14.refs_1_ = bf16[768,512]{1,0:T(8,128)(2,1)S(1)} collective-permute-done((bf16[768,512]{1,0:T(8,128)(2,1)S(1)}, bf16[768,512]{1,0:T(8,128)(2,1)S(1)}, u32[]{:S(2)}, u32[]{:S(2)}) %collective-permute-start.14) | collective-permute-done | bytes 786464 | tf_op jit(solution)/shard_map/ppermute | solution.py:245
  125.5 1.5 %shard_map.73.refs_3_ = bf16[2,768,512]{2,1,0:T(8,128)(2,1)} custom-call(s32[12]{0:T(128)S(1)} %get-tuple-element.21.flags, bf16[768,512]{1,0:T(8,128)(2,1)S(1)} %get-tuple-element.36.refs_0_, bf16[768,512]{1,0:T(8,128)(2,1)S(1)} %collective-permute-done.14.refs_1_, bf16[768,512]{1,0:T(8,128)(2,1)S(1)} %collective-permute-done.15.refs_2_, ...), custom_call_target="tpu_custom_call" | custom-call | flops 1179648 | bytes 3145728 | tf_op jit(solution)/shard_map/pallas_call | solution.py:221
  127.0 10.0 %collective-permute-done.12.refs_1_ = bf16[768,512]{1,0:T(8,128)(2,1)S(1)} collective-permute-done((bf16[768,512]{1,0:T(8,128)(2,1)S(1)}, bf16[768,512]{1,0:T(8,128)(2,1)S(1)}, u32[]{:S(2)}, u32[]{:S(2)}) %collective-permute-start.12) | collective-permute-done | bytes 786464 | tf_op jit(solution)/shard_map/ppermute | solution.py:245
  137.0 1.5 %shard_map.74 = bf16[2,768,512]{2,1,0:T(8,128)(2,1)} custom-call(s32[12]{0:T(128)S(1)} %get-tuple-element.21.flags, bf16[768,512]{1,0:T(8,128)(2,1)S(1)} %get-tuple-element.34.refs_0_, bf16[768,512]{1,0:T(8,128)(2,1)S(1)} %collective-permute-done.12.refs_1_, bf16[768,512]{1,0:T(8,128)(2,1)S(1)} %collective-permute-done.13.refs_2_, ...), custom_call_target="tpu_custom_call", output_to_operand_aliasing={{}: (4, {})} | custom-call | flops 1179648 | bytes 3145728 | tf_op jit(solution)/shard_map/pallas_call | solution.py:221
  (20 shorter events, 0.5 us)
Async XLA Ops:
  0.7 2.2 %copy-start = (bf16[1024,2048]{1,0:T(8,128)(2,1)S(1)}, bf16[1024,2048]{1,0:T(8,128)(2,1)}, u32[]{:S(2)}) copy-start(bf16[1024,2048]{1,0:T(8,128)(2,1)} %grad.13) | copy-start | bytes 12582916
  2.8 1.4 %copy-start.2 = (bf16[1024,768]{1,0:T(8,128)(2,1)S(1)}, bf16[1024,768]{1,0:T(8,128)(2,1)}, u32[]{:S(2)}) copy-start(bf16[1024,768]{1,0:T(8,128)(2,1)} %hidden.13) | copy-start | bytes 4718596
  4.2 0.7 copy-start.4
  4.9 0.7 copy-start.5
  5.6 2.2 %copy-start.1 = (bf16[1024,2048]{1,0:T(8,128)(2,1)S(1)}, bf16[1024,2048]{1,0:T(8,128)(2,1)}, u32[]{:S(2)}) copy-start(bf16[1024,2048]{1,0:T(8,128)(2,1)} %grad.13) | copy-start | bytes 12582916
  9.6 12.1 %collective-permute-start.1 = (bf16[768,512]{1,0:T(8,128)(2,1)S(1)}, bf16[768,512]{1,0:T(8,128)(2,1)S(1)}, u32[]{:S(2)}, u32[]{:S(2)}) collective-permute-start(bf16[768,512]{1,0:T(8,128)(2,1)S(1)} %shard_map.56.refs_0_), channel_id=1, source_target_pairs={{0,2},{1,5},{2,0},{3,7},{4,6},{5,1},{6,4},{7,3},{8,10},{9,13},{10,... | collective-permute-start | bytes 2359304 | tf_op jit(solution)/shard_map/ppermute | solution.py:239
  10.8 21.2 %collective-permute-start.4 = (bf16[768,512]{1,0:T(8,128)(2,1)S(1)}, bf16[768,512]{1,0:T(8,128)(2,1)S(1)}, u32[]{:S(2)}, u32[]{:S(2)}) collective-permute-start(bf16[768,512]{1,0:T(8,128)(2,1)S(1)} %get-tuple-element.22.refs_0_), channel_id=1, source_target_pairs={{0,8},{24,16},{1,9},{25,17},{2,10},{26,18},{3,11},{27,19},{4,12},{... | collective-permute-start | bytes 2359304 | tf_op jit(solution)/shard_map/ppermute | solution.py:242
  21.7 2.4 %copy-start.3 = (bf16[1024,768]{1,0:T(8,128)(2,1)S(1)}, bf16[1024,768]{1,0:T(8,128)(2,1)}, u32[]{:S(2)}) copy-start(bf16[1024,768]{1,0:T(8,128)(2,1)} %hidden.13) | copy-start | bytes 4718596
  22.5 18.8 %collective-permute-start.3 = (bf16[768,512]{1,0:T(8,128)(2,1)S(1)}, bf16[768,512]{1,0:T(8,128)(2,1)S(1)}, u32[]{:S(2)}, u32[]{:S(2)}) collective-permute-start(bf16[768,512]{1,0:T(8,128)(2,1)S(1)} %shard_map.58.refs_0_), channel_id=1, source_target_pairs={{0,4},{1,3},{2,6},{3,1},{4,0},{5,7},{6,2},{7,5},{8,12},{9,11},{10,... | collective-permute-start | bytes 2359304 | tf_op jit(solution)/shard_map/ppermute | solution.py:239
  26.8 21.8 %collective-permute-start.2 = (bf16[768,512]{1,0:T(8,128)(2,1)S(1)}, bf16[768,512]{1,0:T(8,128)(2,1)S(1)}, u32[]{:S(2)}, u32[]{:S(2)}) collective-permute-start(bf16[768,512]{1,0:T(8,128)(2,1)S(1)} %get-tuple-element.24.refs_2_.refs_0_), channel_id=1, source_target_pairs={{0,2},{1,5},{2,0},{3,7},{4,6},{5,1},{6,4},{7,3},{8,10},{9,13},{10,... | collective-permute-start | bytes 2359304 | tf_op jit(solution)/shard_map/ppermute | solution.py:239
  45.4 34.0 %collective-permute-start.5 = (bf16[2,768,512]{2,1,0:T(8,128)(2,1)S(1)}, bf16[2,768,512]{2,1,0:T(8,128)(2,1)S(1)}, u32[]{:S(2)}, u32[]{:S(2)}) collective-permute-start(bf16[2,768,512]{2,1,0:T(8,128)(2,1)S(1)} %pad_maximum_fusion), channel_id=1, source_target_pairs={{0,2},{1,5},{2,0},{3,7},{4,6},{5,1},{6,4},{7,3},{8,10},{9,13},{10,... | collective-permute-start | bytes 4718600 | tf_op jit(solution)/shard_map/ppermute | solution.py:239
  47.3 21.6 %collective-permute-start = (bf16[768,512]{1,0:T(8,128)(2,1)S(1)}, bf16[768,512]{1,0:T(8,128)(2,1)S(1)}, u32[]{:S(2)}, u32[]{:S(2)}) collective-permute-start(bf16[768,512]{1,0:T(8,128)(2,1)S(1)} %get-tuple-element.23.refs_2_.refs_0_), channel_id=1, source_target_pairs={{0,8},{24,16},{1,9},{25,17},{2,10},{26,18},{3,11},{27,19},{4,12},{... | collective-permute-start | bytes 2359304 | tf_op jit(solution)/shard_map/ppermute | solution.py:242
  49.4 22.5 %collective-permute-start.6 = (bf16[768,512]{1,0:T(8,128)(2,1)S(1)}, bf16[768,512]{1,0:T(8,128)(2,1)S(1)}, u32[]{:S(2)}, u32[]{:S(2)}) collective-permute-start(bf16[768,512]{1,0:T(8,128)(2,1)S(1)} %shard_map.63.refs_0_), channel_id=1, source_target_pairs={{0,4},{1,3},{2,6},{3,1},{4,0},{5,7},{6,2},{7,5},{8,12},{9,11},{10,... | collective-permute-start | bytes 2359304 | tf_op jit(solution)/shard_map/ppermute | solution.py:239
  53.5 19.3 %collective-permute-start.8 = (bf16[768,512]{1,0:T(8,128)(2,1)S(1)}, bf16[768,512]{1,0:T(8,128)(2,1)S(1)}, u32[]{:S(2)}, u32[]{:S(2)}) collective-permute-start(bf16[768,512]{1,0:T(8,128)(2,1)S(1)} %shard_map.60.refs_3_), channel_id=1, source_target_pairs={{8,16},{16,8},{9,17},{17,9},{10,18},{18,10},{11,19},{19,11},{12,20... | collective-permute-start | bytes 2359304 | tf_op jit(solution)/shard_map/ppermute | solution.py:245
  55.4 23.2 %collective-permute-start.7 = (bf16[768,512]{1,0:T(8,128)(2,1)S(1)}, bf16[768,512]{1,0:T(8,128)(2,1)S(1)}, u32[]{:S(2)}, u32[]{:S(2)}) collective-permute-start(bf16[768,512]{1,0:T(8,128)(2,1)S(1)} %shard_map.61.refs_0_), channel_id=1, source_target_pairs={{0,8},{24,16},{1,9},{25,17},{2,10},{26,18},{3,11},{27,19},{4,12},{... | collective-permute-start | bytes 2359304 | tf_op jit(solution)/shard_map/ppermute | solution.py:242
  80.8 31.2 %collective-permute-start.9 = (bf16[2,768,512]{2,1,0:T(8,128)(2,1)S(1)}, bf16[2,768,512]{2,1,0:T(8,128)(2,1)S(1)}, u32[]{:S(2)}, u32[]{:S(2)}) collective-permute-start(bf16[2,768,512]{2,1,0:T(8,128)(2,1)S(1)} %pad_maximum_fusion.1), channel_id=1, source_target_pairs={{0,4},{1,3},{2,6},{3,1},{4,0},{5,7},{6,2},{7,5},{8,12},{9,11},{10,... | collective-permute-start | bytes 4718600 | tf_op jit(solution)/shard_map/ppermute | solution.py:239
  82.4 22.4 %collective-permute-start.11 = (bf16[768,512]{1,0:T(8,128)(2,1)S(1)}, bf16[768,512]{1,0:T(8,128)(2,1)S(1)}, u32[]{:S(2)}, u32[]{:S(2)}) collective-permute-start(bf16[768,512]{1,0:T(8,128)(2,1)S(1)} %shard_map.67.refs_2_.refs_0_), channel_id=1, source_target_pairs={{0,8},{24,16},{1,9},{25,17},{2,10},{26,18},{3,11},{27,19},{4,12},{... | collective-permute-start | bytes 2359304 | tf_op jit(solution)/shard_map/ppermute | solution.py:242
  83.7 28.4 %collective-permute-start.10 = (bf16[768,512]{1,0:T(8,128)(2,1)S(1)}, bf16[768,512]{1,0:T(8,128)(2,1)S(1)}, u32[]{:S(2)}, u32[]{:S(2)}) collective-permute-start(bf16[768,512]{1,0:T(8,128)(2,1)S(1)} %shard_map.69.refs_4_), channel_id=1, source_target_pairs={{8,16},{16,8},{9,17},{17,9},{10,18},{18,10},{11,19},{19,11},{12,20... | collective-permute-start | bytes 2359304 | tf_op jit(solution)/shard_map/ppermute | solution.py:245
  90.2 35.3 %collective-permute-start.14 = (bf16[768,512]{1,0:T(8,128)(2,1)S(1)}, bf16[768,512]{1,0:T(8,128)(2,1)S(1)}, u32[]{:S(2)}, u32[]{:S(2)}) collective-permute-start(bf16[768,512]{1,0:T(8,128)(2,1)S(1)} %shard_map.65.refs_0_), channel_id=1, source_target_pairs={{8,16},{16,8},{9,17},{17,9},{10,18},{18,10},{11,19},{19,11},{12,20... | collective-permute-start | bytes 2359304 | tf_op jit(solution)/shard_map/ppermute | solution.py:245
  92.1 33.4 %collective-permute-start.15 = (bf16[768,512]{1,0:T(8,128)(2,1)S(1)}, bf16[768,512]{1,0:T(8,128)(2,1)S(1)}, u32[]{:S(2)}, u32[]{:S(2)}) collective-permute-start(bf16[768,512]{1,0:T(8,128)(2,1)S(1)} %shard_map.68.refs_2_), channel_id=1, source_target_pairs={{0,8},{8,0},{16,24},{24,16},{1,9},{9,1},{17,25},{25,17},{2,10},{10... | collective-permute-start | bytes 2359304 | tf_op jit(solution)/shard_map/ppermute | solution.py:248
  105.5 31.5 %collective-permute-start.12 = (bf16[768,512]{1,0:T(8,128)(2,1)S(1)}, bf16[768,512]{1,0:T(8,128)(2,1)S(1)}, u32[]{:S(2)}, u32[]{:S(2)}) collective-permute-start(bf16[768,512]{1,0:T(8,128)(2,1)S(1)} %shard_map.71.refs_7_), channel_id=1, source_target_pairs={{8,16},{16,8},{9,17},{17,9},{10,18},{18,10},{11,19},{19,11},{12,20... | collective-permute-start | bytes 2359304 | tf_op jit(solution)/shard_map/ppermute | solution.py:245
  113.4 23.6 %collective-permute-start.13 = (bf16[768,512]{1,0:T(8,128)(2,1)S(1)}, bf16[768,512]{1,0:T(8,128)(2,1)S(1)}, u32[]{:S(2)}, u32[]{:S(2)}) collective-permute-start(bf16[768,512]{1,0:T(8,128)(2,1)S(1)} %get-tuple-element.35.refs_3_), channel_id=1, source_target_pairs={{0,8},{8,0},{16,24},{24,16},{1,9},{9,1},{17,25},{25,17},{2,10},{10... | collective-permute-start | bytes 2359304 | tf_op jit(solution)/shard_map/ppermute | solution.py:248
